TPU v7x, 512 devices: a whole 4x8x8 slice. The times are simulated.
512 devices in a mesh: dp: 32 (over x_hi, z, core), tensor: 16 (over x_lo, y).
Axes of the slice: x: 4 (x_hi: 2, x_lo: 2; x = x_hi * 2 + x_lo), y: 8, z: 8, core: 2. Of those that a mesh axis runs over, the one named last changes fastest.
Arguments:
- hidden_in: bfloat16 [7680, 4, 5120], P('dp', None, 'tensor'), may hold values from -6 to 6
- kv_weight: bfloat16 [2, 5120, 1024], P(None, 'tensor'), may hold values from -0.078125 to 0.078125
- factor_a: float32 [2, 64, 5120], P(None, None, 'tensor'), may hold values from -0.078125 to 0.078125
- factor_b: float32 [2, 64, 1024], P(None, None, 'tensor'), may hold values from -0.75 to 0.75
- grad_a: float32 [32, 2, 64, 5120], P('dp', None, None, 'tensor'), may hold values from -6 to 6
- grad_b: float32 [32, 2, 64, 1024], P('dp', None, None, 'tensor'), may hold values from -6 to 6
- key_gain: float32 [128], replicated, may hold values from 0.1 to 1.9
- queries: bfloat16 [7680, 4, 4096], P(('dp', 'tensor')), may hold values from -27 to 27
- cache_keys: bfloat16 [7680, 16, 1024], P(('dp', 'tensor')), may hold values from -6 to 6
- cache_values: bfloat16 [7680, 16, 1024], P(('dp', 'tensor')), may hold values from -6 to 6
- cache_lengths: int32 [7680], P(('dp', 'tensor')), may hold values from 2 to 12, as said below
- positions: int32 [7680], P(('dp', 'tensor')), may hold values from 0 to 32767
Outputs:
- attended: bfloat16 [7680, 4, 4096], P(('dp', 'tensor'))
- new_a: float32 [2, 64, 5120], P(None, None, 'tensor')
- new_b: float32 [2, 64, 1024], P(None, None, 'tensor')
Inputs may be any that keep to these rules, and one draw needn't show every extreme that they name: `cache_lengths`: some row holds 12 filled slots.
All inputs are finite; a program needn't handle non-finite values.
Results may differ from a plain program's by a relative error of at most 0.035.
Values may be sent and summed in bfloat16 or wider, within the bound.
A program may use at most 64 MiB of HBM per device.

v0:
```python
import math

import jax
import jax.numpy as jnp
from jax import lax
from jax.sharding import PartitionSpec as P

D = 5120
KVH = 8
HD = 128
QH = 32
R = 64
STEPS = 4


def normed_rotated(keys, gain, position):
    scale = lax.rsqrt(jnp.mean(keys * keys, axis=-1, keepdims=True) + 1e-06)
    keys = keys * scale * gain
    half = keys.shape[-1] // 2
    freq = jnp.exp(
        -math.log(1000000.0) * (jnp.arange(half, dtype=jnp.float32) * 2.0 / keys.shape[-1])
    )
    angle = position.astype(jnp.float32)[..., None] * freq
    cosine = jnp.concatenate([jnp.cos(angle), jnp.cos(angle)], axis=-1)[..., None, :]
    sine = jnp.concatenate([jnp.sin(angle), jnp.sin(angle)], axis=-1)[..., None, :]
    turned = jnp.concatenate([-keys[..., half:], keys[..., :half]], axis=-1)
    return keys * cosine + turned * sine


def attend(queries, cache_keys, cache_values, new_keys, new_values, lengths):
    rows, steps, width = queries.shape
    slots = cache_keys.shape[1]
    slot = jnp.arange(slots, dtype=jnp.int32)
    for step in range(steps):
        hit = (slot[None, :] == lengths[:, None] + step)[:, :, None]
        cache_keys = jnp.where(hit, new_keys[:, step][:, None, :], cache_keys)
        cache_values = jnp.where(hit, new_values[:, step][:, None, :], cache_values)
    groups = QH // KVH
    query_five = queries.reshape(rows, steps, KVH, groups, HD)
    key_four = cache_keys.reshape(rows, slots, KVH, HD)
    value_four = cache_values.reshape(rows, slots, KVH, HD)
    scores = jnp.einsum(
        "rtkgd,rckd->rtkgc", query_five, key_four, preferred_element_type=jnp.float32
    ) * HD ** (-0.5)
    limit = lengths[:, None] + jnp.arange(steps, dtype=jnp.int32)[None, :]
    valid = (slot[None, None, :] <= limit[:, :, None])[:, :, None, None, :]
    scores = jnp.where(valid, scores, jnp.float32(-1e30))
    top = jnp.max(scores, axis=-1, keepdims=True)
    expo = jnp.exp(scores - top)
    weights = (expo / jnp.sum(expo, axis=-1, keepdims=True)).astype(jnp.bfloat16)
    result = jnp.einsum(
        "rtkgc,rckd->rtkgd", weights, value_four, preferred_element_type=jnp.float32
    )
    return result.reshape(rows, steps, width).astype(jnp.bfloat16)


def per_device(
    hidden_in,
    kv_weight,
    factor_a,
    factor_b,
    grad_a,
    grad_b,
    key_gain,
    queries,
    cache_keys,
    cache_values,
    cache_lengths,
    positions,
):
    groups_dp = lax.axis_size("dp")
    rate_a = 2.0 / math.sqrt(groups_dp * D)
    rate_b = 2.0 / math.sqrt(groups_dp * R)
    sum_a, sum_b = (
        lax.psum(grad_a[0].astype(jnp.bfloat16), "dp").astype(jnp.float32),
        lax.psum(grad_b[0].astype(jnp.bfloat16), "dp").astype(jnp.float32),
    )
    new_a = factor_a - rate_a * sum_a
    new_b = factor_b - rate_b * sum_b
    full_b = lax.all_gather(new_b.astype(jnp.bfloat16), "tensor", axis=2, tiled=True).astype(
        new_b.dtype
    )
    delta = jnp.einsum("prd,prk->pdk", new_a, full_b, precision=lax.Precision.HIGHEST)
    merged = (kv_weight.astype(jnp.float32) + 0.25 * delta).astype(jnp.bfloat16)
    joined = jnp.concatenate([merged[0], merged[1]], axis=1)
    rows_here = hidden_in.shape[0] // lax.axis_size("tensor")
    pieces = []
    for step in range(STEPS):
        column = hidden_in[:, step, :]

        def step_term(start, count, column=column):
            return jnp.dot(column, joined, preferred_element_type=jnp.float32)

        pieces.append(
            lax.psum_scatter(
                step_term(jnp.int32(0), rows_here * lax.axis_size("tensor")).astype(jnp.bfloat16),
                "tensor",
                scatter_dimension=0,
                tiled=True,
            ).astype(jnp.float32)
        )
    projected = jnp.stack(pieces, axis=1)
    kv_width = KVH * HD
    place = positions[:, None] + jnp.arange(STEPS, dtype=jnp.int32)[None, :]
    keys = normed_rotated(
        projected[..., :kv_width].reshape(rows_here, STEPS, KVH, HD), key_gain, place
    )
    new_keys = keys.reshape(rows_here, STEPS, kv_width).astype(jnp.bfloat16)
    new_values = projected[..., kv_width:].astype(jnp.bfloat16)
    attended = attend(queries, cache_keys, cache_values, new_keys, new_values, cache_lengths)
    return (attended, new_a, new_b)


def solution(mesh):
    return jax.shard_map(
        per_device,
        mesh=mesh,
        in_specs=(
            P("dp", None, "tensor"),
            P(None, "tensor", None),
            P(None, None, "tensor"),
            P(None, None, "tensor"),
            P("dp", None, None, "tensor"),
            P("dp", None, None, "tensor"),
            P(),
            P(("dp", "tensor"), None, None),
            P(("dp", "tensor"), None, None),
            P(("dp", "tensor"), None, None),
            P(("dp", "tensor")),
            P(("dp", "tensor")),
        ),
        out_specs=(
            P(("dp", "tensor"), None, None),
            P(None, None, "tensor"),
            P(None, None, "tensor"),
        ),
        check_vma=False,
    )
```

profile of v0, /device:TPU:1, one launch (start us, length us, event | category | flops | bytes accessed | tf_op | source)
XLA Modules:
  0.0 347.5 jit_solution(656330244042810565)
XLA Ops:
  7.2 1.7 convert_bitcast_fusion
  9.0 0.7 broadcast_add_fusion.2
  9.6 0.7 iota_add_fusion
  10.3 0.8 convert_element_type.102
  11.3 135.0 %psum.15 = bf16[2,64,64]{1,0,2:T(2,128)(2,1)S(1)} all-reduce(bf16[2,64,64]{1,0,2:T(2,128)(2,1)S(1)} %bitcast.100), channel_id=1, replica_groups=mesh['dp'=32,'tensor'=16] {'dp'}, use_global_device_ids=true, to_apply=%region_1.0 | all-reduce | flops 8192 | bytes 32768 | tf_op jit(solution)/shard_map/psum | solution.py:76
  146.3 0.9 copy.35
  147.2 0.7 add_convert_fusion.1
  148.0 0.7 broadcast_bitcast_fusion
  148.6 0.7 iota_compare_fusion.1
  149.9 29.0 %all_gather.3 = bf16[2,64,1024]{1,0,2:T(2,128)(2,1)S(1)} all-gather(bf16[2,64,64]{1,0,2:T(2,128)(2,1)S(1)} %get-tuple-element.17), channel_id=1, replica_groups=mesh['dp'=32,'tensor'=16] {'tensor'}, dimensions={2}, use_global_device_ids=true | all-gather | bytes 278528 | tf_op jit(solution)/shard_map/all_gather | solution.py:80
  178.9 80.1 %all-reduce.11.cloned.1.call-done = bf16[2,64,320]{2,1,0:T(8,128)(2,1)} async-done(((bf16[2,64,320]{2,1,0:T(8,128)(2,1)}), bf16[2,64,320]{2,1,0:T(8,128)(2,1)}) %all-reduce.11.cloned.1.call-update) | async-done | bytes 81936 | tf_op jit(solution)/shard_map/psum | solution.py:75
  259.0 0.9 multiply_subtract_fusion
  259.9 1.3 add_convert_fusion
  261.4 1.0 copy-done.7
  262.4 0.7 fusion.8
  263.1 0.7 fusion.7
  263.8 0.7 fusion.6
  264.5 1.7 fusion.5
  266.2 49.6 %fusion.30 = (bf16[16,2048]{1,0:T(8,128)(2,1)S(1)}, bf16[16,2048]{1,0:T(8,128)(2,1)S(1)}, bf16[16,2048]{1,0:T(8,128)(2,1)S(1)}, bf16[16,2048]{1,0:T(8,128)(2,1)S(1)}) fusion(bf16[240,2048]{1,0:T(8,128)(2,1)} %fusion.5, bf16[240,2048]{1,0:T(8,128)(2,1)S(1)} %fusion.6, bf16[240,2048]{1,0:T(8,128)(2,1)S(1)} %fusion.7, bf16[240,2048]{1,0:T(8,128)(2,1)S(1)} %fusion.8), kind=kCustom, calls=%all-reduce-scatter.4 | all-reduce-scatter fusion | flops 2097153 | bytes 4196352
  315.8 2.4 collective-permute-start
  318.4 0.5 reshape.181
  318.9 0.7 copy.45
  319.7 1.3 dynamic-slice.10
  321.6 2.4 collective-permute-start.1
  324.0 3.5 %collective-permute-start.2 = (bf16[15,2048]{1,0:T(8,128)(2,1)S(1)}, bf16[15,2048]{1,0:T(8,128)(2,1)S(1)}, u32[]{:S(2)}, u32[]{:S(2)}) collective-permute-start(bf16[15,2048]{1,0:T(8,128)(2,1)S(1)} %slice.96), channel_id=1, source_target_pairs={{0,1},{1,2},{2,3},{3,4},{4,5},{5,6},{6,7},{7,8},{8,9},{9,10},{10,1... | collective-permute-start | bytes 184328
  327.6 5.3 %collective-permute-start.3 = (bf16[15,2048]{1,0:T(8,128)(2,1)S(1)}, bf16[15,2048]{1,0:T(8,128)(2,1)S(1)}, u32[]{:S(2)}, u32[]{:S(2)}) collective-permute-start(bf16[15,2048]{1,0:T(8,128)(2,1)S(1)} %slice.97), channel_id=1, source_target_pairs={{0,1},{1,2},{2,3},{3,4},{4,5},{5,6},{6,7},{7,8},{8,9},{9,10},{10,1... | collective-permute-start | bytes 184328
  333.7 0.5 collective-permute-done.3
  335.5 0.4 fusion.19
  336.3 0.4 select_select_fusion.1
  337.0 1.6 fusion.32
  338.6 0.9 fusion.13
  339.8 0.9 convert_element_type.101
  (60 shorter events, 3.8 us)
Async XLA Ops:
  7.2 251.8 %copy-start.5 = (f32[2,64,320]{2,1,0:T(8,128)S(1)}, f32[2,64,320]{2,1,0:T(8,128)}, u32[]{:S(2)}) copy-start(f32[2,64,320]{2,1,0:T(8,128)} %param.14) | copy-start | bytes 491524
  7.2 252.7 %copy-start = (bf16[2,320,1024]{2,1,0:T(8,128)(2,1)S(1)}, bf16[2,320,1024]{2,1,0:T(8,128)(2,1)}, u32[]{:S(2)}) copy-start(bf16[2,320,1024]{2,1,0:T(8,128)(2,1)} %param.13) | copy-start | bytes 3932164
  7.2 251.8 %all-reduce.11.cloned.1.call-start = ((), (), s32[]{:S(2)}) async-start(), calls=%async_computation | async-start | bytes 196608 | tf_op jit(solution)/shard_map/psum | solution.py:75
  259.9 1.4 copy-start.1
  261.3 1.1 copy-start.7
  315.8 2.7 copy-start.2
  315.8 17.1 %collective-permute-start = (bf16[15,2048]{1,0:T(8,128)(2,1)S(1)}, bf16[15,2048]{1,0:T(8,128)(2,1)S(1)}, u32[]{:S(2)}, u32[]{:S(2)}) collective-permute-start(bf16[15,2048]{1,0:T(8,128)(2,1)S(1)} %slice.94), channel_id=1, source_target_pairs={{0,1},{1,2},{2,3},{3,4},{4,5},{5,6},{6,7},{7,8},{8,9},{9,10},{10,1... | collective-permute-start | bytes 184328
  321.6 11.5 %collective-permute-start.1 = (bf16[15,2048]{1,0:T(8,128)(2,1)S(1)}, bf16[15,2048]{1,0:T(8,128)(2,1)S(1)}, u32[]{:S(2)}, u32[]{:S(2)}) collective-permute-start(bf16[15,2048]{1,0:T(8,128)(2,1)S(1)} %slice.95), channel_id=1, source_target_pairs={{0,1},{1,2},{2,3},{3,4},{4,5},{5,6},{6,7},{7,8},{8,9},{9,10},{10,1... | collective-permute-start | bytes 184328
  324.0 9.4 %collective-permute-start.2 = (bf16[15,2048]{1,0:T(8,128)(2,1)S(1)}, bf16[15,2048]{1,0:T(8,128)(2,1)S(1)}, u32[]{:S(2)}, u32[]{:S(2)}) collective-permute-start(bf16[15,2048]{1,0:T(8,128)(2,1)S(1)} %slice.96), channel_id=1, source_target_pairs={{0,1},{1,2},{2,3},{3,4},{4,5},{5,6},{6,7},{7,8},{8,9},{9,10},{10,1... | collective-permute-start | bytes 184328
  327.6 6.6 %collective-permute-start.3 = (bf16[15,2048]{1,0:T(8,128)(2,1)S(1)}, bf16[15,2048]{1,0:T(8,128)(2,1)S(1)}, u32[]{:S(2)}, u32[]{:S(2)}) collective-permute-start(bf16[15,2048]{1,0:T(8,128)(2,1)S(1)} %slice.97), channel_id=1, source_target_pairs={{0,1},{1,2},{2,3},{3,4},{4,5},{5,6},{6,7},{7,8},{8,9},{9,10},{10,1... | collective-permute-start | bytes 184328
  333.4 1.4 copy-start.6
  335.2 1.0 copy-start.3
  335.2 1.2 copy-start.4
Sparse Core Ops, SparseCore 0:
  11.5 247.4 all-reduce.10
where the time goes:
time: 352 us; the launch traced here: 348 us
  blocking collectives  214 us (61%)
  waiting for transfers between devices  80.6 us (23%)
  between operations  15.2 us (4%)
  starting transfers between devices  13.6 us (4%)
  local copies, waits for them, and re-layouts  8.51 us (2%)
  other arithmetic  8.36 us (2%)
  matrix products  7.64 us (2%)
    psum x1, blocking collectives, per_device(): lax.psum(grad_b[0].astype(jnp.bfloat16), 'dp').astype(jnp.float32)  135 us
    psum x1, waiting for transfers between devices, per_device(): lax.psum(grad_a[0].astype(jnp.bfloat16), 'dp').astype(jnp.float32)  80.1 us
    unnamed x1, blocking collectives  49.6 us
    all_gather x1, blocking collectives, per_device(): lax.all_gather(new_b.astype(jnp.bfloat16), 'tensor', axis=2, tiled=True)  29 us
    unnamed x4, starting transfers between devices  13.6 us
  transfers between devices with their start and end apart: 5, of which 2 were waited for; matrix products, arithmetic and copies ran while one was open for 3% of the time, Pallas kernels for 0%

commit v1 on v0

--- a/solution.py
+++ b/solution.py
@@ -3,6 +3,8 @@
 import jax
 import jax.numpy as jnp
 from jax import lax
+from jax.experimental import pallas as pl
+from jax.experimental.pallas import tpu as pltpu
 from jax.sharding import PartitionSpec as P
 
 D = 5120
@@ -11,6 +13,362 @@
 QH = 32
 R = 64
 STEPS = 4
+KV = 2048
+MESH = pl.DeviceIdType.MESH
+
+NY = 8
+NZ = 8
+TOK = 64
+DS = 320
+NC = 4
+CW = 512
+HALF = CW // 2
+ORDER = (4, 3, 5, 2, 6, 1, 7, 0)
+GR = 384
+GH = GR // 2
+GZ = GH // NZ
+F32 = jnp.float32
+BF = jnp.bfloat16
+
+
+def transfer_kernel(
+    rate_a, rate_b,
+    hb, kv, ga, gb, fa, fb,
+    proj, na, nb,
+    hown, hrem, wown, wrem, pk,
+    sb0, rb0, sb, rb, pu, sbu, rbu,
+    tpad, gT, g1s, g1r, g2s, g2r, h2, g3r, tot, naown, narem, nbt, nball,
+    loc, ssem, rsem,
+):
+    dp = lax.axis_index("dp")
+    tn = lax.axis_index("tensor")
+    xh, z, c = dp // 16, lax.rem(dp // 2, 8), lax.rem(dp, 2)
+    a, y = tn // NY, lax.rem(tn, NY)
+    dsib = dp + 1 - 2 * c
+    dflip = lax.rem(dp + 16, 32)
+    tflip = lax.rem(tn + 8, 16)
+    sib = (dsib, tn)
+    xflip = (dflip, tn)
+    part = (dp, tflip)
+    other = (dflip, tflip)
+    partsib = (dsib, tflip)
+    up = (dp, a * NY + lax.rem(y + 1, NY))
+    down = (dp, a * NY + lax.rem(y + NY - 1, NY))
+    zpeer = [None] + [(xh * 16 + lax.rem(z + i, NZ) * 2 + c, tn) for i in range(1, NZ)]
+    ring = (up, down)
+    peers = [sib, xflip, part, other, partsib, up, down] + zpeer[1:]
+
+    barrier = pltpu.get_barrier_semaphore()
+    for peer in peers:
+        pl.semaphore_signal(barrier, inc=1, device_id=peer, device_id_type=MESH)
+
+    def block(side, j):
+        row = (side * NY + lax.rem(y + j, NY)) * TOK
+        return hb.at[pl.ds(pl.multiple_of(row, TOK), TOK)]
+
+    lh = []
+    for i, j in enumerate(ORDER):
+        cp = pltpu.make_async_copy(block(a, j), hown.at[pl.ds(i * TOK, TOK)], loc.at[i])
+        cp.start()
+        lh.append(cp)
+    lw = []
+    for k in range(NC):
+        cols = pl.ds((k % 2) * CW, CW)
+        cp = pltpu.make_async_copy(kv.at[k // 2, :, cols], wown.at[k // 2, :, cols], loc.at[8 + k])
+        cp.start()
+        lw.append(cp)
+
+    count = [0]
+    started = []
+
+    def remote(src, dst, device):
+        i = count[0]
+        count[0] += 1
+        cp = pltpu.make_async_remote_copy(
+            src_ref=src, dst_ref=dst, send_sem=ssem.at[i], recv_sem=rsem.at[i],
+            device_id=device, device_id_type=MESH,
+        )
+        cp.start()
+        started.append(cp)
+        return cp
+
+    tpad[...] = jnp.zeros_like(tpad)
+    tpad[:, 0:DS] = ga[...]
+    gT[...] = tpad[...].T
+    tpad[:, 0:R] = gb[...]
+    gT[DS:GR, :] = tpad[:, 0:128].T[0:R, :]
+
+    pl.semaphore_wait(barrier, len(peers))
+
+    krow = c * (DS // 2)
+
+    def weight(k, lo, n, device):
+        rows = pl.ds(pl.multiple_of(krow + lo, 16), n)
+        cols = pl.ds((k % 2) * CW, CW)
+        return remote(kv.at[k // 2, rows, cols], wrem.at[k // 2, rows, cols], device)
+
+    def forward(k):
+        rows = pl.ds(pl.multiple_of(krow, 16), DS // 2)
+        cols = pl.ds((k % 2) * CW, CW)
+        ref = wrem.at[k // 2, rows, cols]
+        return remote(ref, ref, sib)
+
+    def hidden(i):
+        return remote(block(1 - a, ORDER[i]), hrem.at[pl.ds(i * TOK, TOK)], part)
+
+    w0a = weight(0, 0, 80, part)
+    w0b = weight(0, 80, 80, other)
+    mine = pl.multiple_of(c * GH, GH)
+    theirs = pl.multiple_of((1 - c) * GH, GH)
+    g1s[...] = gT[pl.ds(theirs, GH), :].astype(BF)
+    g1 = remote(g1s, g1r, sib)
+    hr = [hidden(i) for i in range(5)]
+    w1 = weight(1, 0, 160, other)
+    hr += [hidden(i) for i in range(5, 8)]
+    w2 = weight(2, 0, 160, other)
+    w3 = weight(3, 0, 160, part)
+
+    def product(k, lo, n):
+        cols = slice((k % 2) * CW, (k % 2) * CW + CW)
+        pk[k, lo:lo + n, :] = jnp.dot(
+            hown[lo:lo + n, :], wown[k // 2, :, cols], preferred_element_type=F32
+        ) + jnp.dot(hrem[lo:lo + n, :], wrem[k // 2, :, cols], preferred_element_type=F32)
+
+    sent = {}
+
+    def stage(k, s):
+        if s == 0:
+            for way in range(2):
+                cut = slice(way * HALF, way * HALF + HALF)
+                sb0[k, way] = pk[k, 0:TOK, cut].astype(BF)
+                sent[k, 0, way] = remote(sb0.at[k, way], rb0.at[k, way], ring[way])
+            return
+        for way in range(2):
+            lo = (2 * s - 1 + way) * TOK
+            sent[k, s - 1, way].wait_recv()
+            if s == 1:
+                cut = slice(way * HALF, way * HALF + HALF)
+                rest = slice((1 - way) * HALF, (1 - way) * HALF + HALF)
+                sb[k, 0, way, :, cut] = (
+                    pk[k, lo:lo + TOK, cut] + rb0[k, way].astype(F32)
+                ).astype(BF)
+                sb[k, 0, way, :, rest] = pk[k, lo:lo + TOK, rest].astype(BF)
+            else:
+                sb[k, s - 1, way] = (
+                    pk[k, lo:lo + TOK, :] + rb[k, s - 2, way].astype(F32)
+                ).astype(BF)
+            sent[k, s, way] = remote(sb.at[k, s - 1, way], rb.at[k, s - 1, way], ring[way])
+
+    def last(k):
+        for way in range(2):
+            sent[k, 3, way].wait_recv()
+        proj[:, k * CW:(k + 1) * CW] = (
+            pk[k, 7 * TOK:, :] + rb[k, 2, 0].astype(F32) + rb[k, 2, 1].astype(F32)
+        )
+
+    usent = {}
+
+    def ustage(s):
+        if s == 0:
+            sbu[0, 0] = pu[0:TOK, :].astype(BF)
+            usent[0, 0] = remote(sbu.at[0, 0], rbu.at[0, 0], up)
+            return
+        for way in range(2):
+            lo = (2 * s - 1 + way) * TOK
+            total = pu[lo:lo + TOK, :]
+            if s > 1 or way == 0:
+                usent[s - 1, way].wait_recv()
+                total = total + rbu[s - 1, way].astype(F32)
+            sbu[s, way] = total.astype(BF)
+            usent[s, way] = remote(sbu.at[s, way], rbu.at[s, way], ring[way])
+
+    bsent = {}
+    bcols = pl.ds(pl.multiple_of(c * 32, 32), 32)
+
+    def bstage(s):
+        if s > 0:
+            bsent[s - 1, 0].wait_recv()
+            if s < 3:
+                bsent[s - 1, 1].wait_recv()
+        for way in range(2 if s < 3 else 1):
+            from_y = lax.rem(y + NY - s, NY) if way == 0 else lax.rem(y + s, NY)
+            ref = nball.at[a * NY + from_y, bcols, :]
+            bsent[s, way] = remote(ref, ref, ring[way])
+
+    w0a.wait_recv()
+    w0b.wait_recv()
+    f0 = forward(0)
+    g1.wait_recv()
+    g2s[...] = (gT[pl.ds(mine, GH), :] + g1r[...].astype(F32)).astype(BF)
+    g2 = remote(g2s, g2r, xflip)
+    lw[0].wait()
+    lh[0].wait()
+    hr[0].wait_recv()
+    f0.wait_recv()
+    product(0, 0, TOK)
+    stage(0, 0)
+    for i in (1, 2):
+        lh[i].wait()
+        hr[i].wait_recv()
+    product(0, TOK, 2 * TOK)
+
+    stage(0, 1)
+    g2.wait_recv()
+    h2[...] = g2s[...].astype(F32) + g2r[...].astype(F32)
+    g3 = []
+    for i in range(1, NZ):
+        rows = pl.ds(pl.multiple_of(lax.rem(z + i, NZ) * GZ, GZ), GZ)
+        g3.append(remote(h2.at[rows, :], g3r.at[i], zpeer[i]))
+    w1.wait_recv()
+    f1 = forward(1)
+    for i in range(3, 8):
+        lh[i].wait()
+        hr[i].wait_recv()
+    product(0, 3 * TOK, 5 * TOK)
+    lw[1].wait()
+    f1.wait_recv()
+    product(1, 0, 8 * TOK)
+    stage(1, 0)
+
+    stage(0, 2)
+    stage(1, 1)
+    total = h2[pl.ds(pl.multiple_of(z * GZ, GZ), GZ), :]
+    for i in range(1, NZ):
+        g3[i - 1].wait_recv()
+        total = total + g3r[i]
+    piece = pl.ds(pl.multiple_of(c * GH + z * GZ, GZ), GZ)
+    tot[piece, :] = total
+    g4 = [remote(tot.at[piece, :], tot.at[piece, :], zpeer[i]) for i in range(1, NZ)]
+    w2.wait_recv()
+    f2 = forward(2)
+    lw[2].wait()
+    f2.wait_recv()
+    product(2, 0, 8 * TOK)
+    stage(2, 0)
+
+    stage(0, 3)
+    stage(1, 2)
+    stage(2, 1)
+    for cp in g4:
+        cp.wait_recv()
+    half = tot.at[pl.ds(mine, GH), :]
+    g5 = remote(half, half, sib)
+    w3.wait_recv()
+    f3 = forward(3)
+    lw[3].wait()
+    f3.wait_recv()
+    product(3, 0, 8 * TOK)
+    stage(3, 0)
+    tpad[:, 0:DS] = fa[...]
+    faT = tpad[...].T[0:DS, :]
+    tpad[:, 0:R] = fb[...]
+    fbT = tpad[:, 0:128].T[0:R, :]
+    g5.wait_recv()
+    naown[...] = (faT - rate_a * tot[0:DS, :]).astype(BF)
+    n1 = remote(naown, narem, part)
+    nbt[...] = fbT - rate_b * tot[DS:GR, :]
+    nball[tn, bcols, :] = nbt[bcols, :].astype(BF)
+    bstage(0)
+
+    last(0)
+    stage(1, 3)
+    stage(2, 2)
+    stage(3, 1)
+    n1.wait_recv()
+    pu[...] = jnp.dot(hown[...], naown[...], preferred_element_type=F32) + jnp.dot(
+        hrem[...], narem[...], preferred_element_type=F32
+    )
+    ustage(0)
+    bstage(1)
+    back = tot[...].T
+    na[...] = fa[...] - rate_a * back[:, 0:DS]
+    nb[...] = fb[...] - rate_b * back[:, DS:GR]
+
+    last(1)
+    stage(2, 3)
+    stage(3, 2)
+    bstage(2)
+    ustage(1)
+
+    last(2)
+    stage(3, 3)
+    ustage(2)
+    bstage(3)
+    ustage(3)
+
+    bsent[3, 0].wait_recv()
+    bsent[2, 1].wait_recv()
+    mineb = nball.at[pl.ds(pl.multiple_of(a * NY, NY), NY), bcols, :]
+    shared = [remote(mineb, mineb, device) for device in (sib, part, partsib)]
+    last(3)
+    for way in range(2):
+        usent[3, way].wait_recv()
+    u = (pu[7 * TOK:, :] + rbu[3, 0].astype(F32) + rbu[3, 1].astype(F32)) * 0.25
+    lane = lax.broadcasted_iota(jnp.int32, u.shape, 1)
+    for cp in shared:
+        cp.wait_recv()
+    allb = nball[...].reshape(16 * R, 128)
+    for p in range(2):
+        up_ = jnp.where((lane >= p * R) & (lane < p * R + R), u, 0.0).astype(BF)
+        proj[:, p * 1024:(p + 1) * 1024] += lax.dot_general(
+            up_, allb, (((1,), (1,)), ((), ())), preferred_element_type=F32
+        )
+    for cp in started:
+        cp.wait_send()
+
+
+N_REMOTE = 5 + 4 + 8 + 32 + 7 + 2 + 7 + 7 + 1 + 1 + 7 + 3
+
+
+def transfers(rate_a, rate_b, hb, kv, ga, gb, fa, fb):
+    def body(*refs):
+        transfer_kernel(rate_a, rate_b, *refs)
+
+    vmem = pl.BlockSpec(memory_space=pltpu.VMEM)
+    hbm = pl.BlockSpec(memory_space=pl.ANY)
+    return pl.pallas_call(
+        body,
+        out_shape=(
+            jax.ShapeDtypeStruct((TOK, KV), F32),
+            jax.ShapeDtypeStruct((2 * R, DS), F32),
+            jax.ShapeDtypeStruct((2 * R, R), F32),
+        ),
+        in_specs=[hbm, hbm, vmem, vmem, vmem, vmem],
+        out_specs=(vmem, vmem, vmem),
+        scratch_shapes=[
+            pltpu.VMEM((8 * TOK, DS), BF),
+            pltpu.VMEM((8 * TOK, DS), BF),
+            pltpu.VMEM((2, DS, 1024), BF),
+            pltpu.VMEM((2, DS, 1024), BF),
+            pltpu.VMEM((NC, 8 * TOK, CW), F32),
+            pltpu.VMEM((NC, 2, TOK, HALF), BF),
+            pltpu.VMEM((NC, 2, TOK, HALF), BF),
+            pltpu.VMEM((NC, 3, 2, TOK, CW), BF),
+            pltpu.VMEM((NC, 3, 2, TOK, CW), BF),
+            pltpu.VMEM((8 * TOK, 128), F32),
+            pltpu.VMEM((4, 2, TOK, 128), BF),
+            pltpu.VMEM((4, 2, TOK, 128), BF),
+            pltpu.VMEM((128, GR), F32),
+            pltpu.VMEM((GR, 128), F32),
+            pltpu.VMEM((GH, 128), BF),
+            pltpu.VMEM((GH, 128), BF),
+            pltpu.VMEM((GH, 128), BF),
+            pltpu.VMEM((GH, 128), BF),
+            pltpu.VMEM((GH, 128), F32),
+            pltpu.VMEM((NZ, GZ, 128), F32),
+            pltpu.VMEM((GR, 128), F32),
+            pltpu.VMEM((DS, 128), BF),
+            pltpu.VMEM((DS, 128), BF),
+            pltpu.VMEM((R, 128), F32),
+            pltpu.VMEM((16, R, 128), BF),
+            pltpu.SemaphoreType.DMA((12,)),
+            pltpu.SemaphoreType.DMA((N_REMOTE,)),
+            pltpu.SemaphoreType.DMA((N_REMOTE,)),
+        ],
+        compiler_params=pltpu.CompilerParams(
+            collective_id=0, has_side_effects=True, vmem_limit_bytes=48 * 1024 * 1024
+        ),
+    )(hb, kv, ga, gb, fa, fb)
 
 
 def normed_rotated(keys, gain, position):
@@ -55,51 +413,22 @@
 
 
 def per_device(
-    hidden_in,
-    kv_weight,
-    factor_a,
-    factor_b,
-    grad_a,
-    grad_b,
-    key_gain,
-    queries,
-    cache_keys,
-    cache_values,
-    cache_lengths,
-    positions,
+    hidden_in, kv_weight, factor_a, factor_b, grad_a, grad_b, key_gain,
+    queries, cache_keys, cache_values, cache_lengths, positions,
 ):
     groups_dp = lax.axis_size("dp")
     rate_a = 2.0 / math.sqrt(groups_dp * D)
     rate_b = 2.0 / math.sqrt(groups_dp * R)
-    sum_a, sum_b = (
-        lax.psum(grad_a[0].astype(jnp.bfloat16), "dp").astype(jnp.float32),
-        lax.psum(grad_b[0].astype(jnp.bfloat16), "dp").astype(jnp.float32),
-    )
-    new_a = factor_a - rate_a * sum_a
-    new_b = factor_b - rate_b * sum_b
-    full_b = lax.all_gather(new_b.astype(jnp.bfloat16), "tensor", axis=2, tiled=True).astype(
-        new_b.dtype
-    )
-    delta = jnp.einsum("prd,prk->pdk", new_a, full_b, precision=lax.Precision.HIGHEST)
-    merged = (kv_weight.astype(jnp.float32) + 0.25 * delta).astype(jnp.bfloat16)
-    joined = jnp.concatenate([merged[0], merged[1]], axis=1)
-    rows_here = hidden_in.shape[0] // lax.axis_size("tensor")
-    pieces = []
-    for step in range(STEPS):
-        column = hidden_in[:, step, :]
-
-        def step_term(start, count, column=column):
-            return jnp.dot(column, joined, preferred_element_type=jnp.float32)
-
-        pieces.append(
-            lax.psum_scatter(
-                step_term(jnp.int32(0), rows_here * lax.axis_size("tensor")).astype(jnp.bfloat16),
-                "tensor",
-                scatter_dimension=0,
-                tiled=True,
-            ).astype(jnp.float32)
-        )
-    projected = jnp.stack(pieces, axis=1)
+    rows_here = queries.shape[0]
+    hb = jnp.pad(hidden_in.reshape(16, rows_here * STEPS, DS), ((0, 0), (0, 4), (0, 0)))
+    proj, na, nb = transfers(
+        rate_a, rate_b, hb.reshape(16 * TOK, DS), kv_weight,
+        grad_a.reshape(2 * R, DS), grad_b.reshape(2 * R, R),
+        factor_a.reshape(2 * R, DS), factor_b.reshape(2 * R, R),
+    )
+    new_a = na.reshape(2, R, DS)
+    new_b = nb.reshape(2, R, R)
+    projected = proj[:rows_here * STEPS].reshape(rows_here, STEPS, KV)
     kv_width = KVH * HD
     place = positions[:, None] + jnp.arange(STEPS, dtype=jnp.int32)[None, :]
     keys = normed_rotated(

time: 352 us -> 84.8 us (0.24); the launches traced: 348 us -> 84.5 us
  blocking collectives: 214 us -> 0 us
  waiting for transfers between devices: 80.6 us -> 0 us
  Pallas kernels: 0 us -> 64.9 us
  between operations: 15.2 us -> 0.97 us
  starting transfers between devices: 13.6 us -> 0 us
  matrix products: 7.64 us -> 2.5 us
  other arithmetic: 8.36 us -> 4.68 us
    psum x1 -> x0, blocking collectives: 135 us -> none  [per_device(): lax.psum(grad_b[0].astype(jnp.bfloat16), 'dp').astype(jnp.float32)]
    psum x1 -> x0, waiting for transfers between devices: 80.1 us -> none  [per_device(): lax.psum(grad_a[0].astype(jnp.bfloat16), 'dp').astype(jnp.float32)]
    pallas_call x0 -> x1, Pallas kernels: none -> 64.9 us  [transfers(): pl.pallas_call(body, out_shape=(jax.ShapeDtypeStruct((TOK, KV), F32), jax...]
    unnamed x1 -> x0, blocking collectives: 49.6 us -> none
    all_gather x1 -> x0, blocking collectives: 29 us -> none  [per_device(): lax.all_gather(new_b.astype(jnp.bfloat16), 'tensor', axis=2, tiled=True)]
    unnamed x4 -> x0, starting transfers between devices: 13.6 us -> none
    dot_general x5 -> x0, matrix products: 5.14 us -> none  [the longest x4 3.8 us: step_term(): return jnp.dot(column, joined, preferred_element_type=jnp.float32)]
  transfers between devices with their start and end apart: 5 -> 0, of which waited for: 2 -> 0; matrix products, arithmetic and copies ran while one was open for 3% -> 0% of each run, Pallas kernels for 0% -> 0%
where the time goes in v1:
time: 84.8 us; the launch traced here: 84.5 us
  Pallas kernels  64.9 us (77%)
  local copies, waits for them, and re-layouts  11.5 us (14%)
  other arithmetic  4.68 us (6%)
  matrix products  2.5 us (3%)
  between operations  0.97 us (1%)
    pallas_call x1, Pallas kernels, transfers(): pl.pallas_call(body, out_shape=(jax.ShapeDtypeStruct((TOK, KV), F32), jax...  64.9 us
    unnamed x33, local copies, waits for them, and re-layouts  4.79 us

profile of v1, /device:TPU:1, one launch (start us, length us, event | category | flops | bytes accessed | tf_op | source)
XLA Modules:
  0.0 84.5 jit_solution(11505160440894577357)
XLA Ops:
  0.7 0.7 broadcast_add_fusion.2
  1.4 0.7 iota_compare_fusion.1
  2.1 0.7 broadcast_bitcast_fusion
  2.9 0.7 add_convert_fusion.1
  3.6 0.7 iota_add_fusion
  4.4 0.3 multiply_cosine_fusion
  4.9 0.8 mul.105
  5.6 1.3 %reshape.213 = bf16[15,4,8,4,128]{4,3,2,1,0:T(4,128)(2,1)} reshape(bf16[15,4,4096]{2,1,0:T(4,128)(2,1)S(1)} %copy-done.7) | data formatting | bytes 983040 | tf_op jit(solution)/shard_map/reshape | solution.py:397
  6.9 1.3 %copy.25 = bf16[240,4,320]{2,1,0:T(4,128)(2,1)} copy(bf16[240,4,320]{0,2,1:T(8,128)(2,1)S(1)} %copy-done.6) | data formatting | bytes 1228800 | tf_op args[0]
  8.2 1.7 %reshape.203 = bf16[16,60,320]{2,1,0:T(8,128)(2,1)S(1)} reshape(bf16[240,4,320]{2,1,0:T(4,128)(2,1)} %copy.25) | data formatting | bytes 1228800 | tf_op jit(solution)/shard_map/reshape | solution.py:423
  10.1 64.9 %shard_map.139 = (f32[64,2048]{1,0:T(8,128)S(1)}, f32[128,320]{1,0:T(8,128)S(1)}, f32[128,64]{1,0:T(8,128)S(1)}) custom-call(bf16[1024,320]{1,0:T(8,128)(2,1)S(1)} %bitcast.60, bf16[2,320,1024]{2,1,0:T(8,128)(2,1)S(1)} %copy-done, f32[128,320]{1,0:T(8,128)S(1)} %bitcast.62, f32[128,64]{1,0:T(8,128)S(1)} %bitcast.65, f32[128,320]{1,0:T(8,128)S(1)} %bitcast.63, ...), custom_call_target="tpu_custom_call" | custom-call | tf_op jit(solution)/shard_map/pallas_call | solution.py:329
  75.0 0.1 reshape.209
  75.2 0.2 multiply_reduce_fusion
  75.4 0.2 copy-done.11
  75.6 0.1 multiply_multiply_fusion
  75.7 0.1 mul.92
  76.0 0.1 slice_negate_fusion
  76.1 0.1 maximum_multiply_fusion
  76.3 0.5 copy-done.5
  76.8 0.2 add_convert_fusion
  77.0 0.3 copy.54
  77.3 0.2 fusion.10
  77.5 0.3 copy-done.8
  77.8 0.1 copy-done.9
  78.0 0.5 select_select_fusion.1
  78.7 0.8 %copy-done.10 = bf16[15,4,8,4,128]{4,3,2,1,0:T(4,128)(2,1)S(1)} copy-done((bf16[15,4,8,4,128]{4,3,2,1,0:T(4,128)(2,1)S(1)}, bf16[15,4,8,4,128]{4,3,2,1,0:T(4,128)(2,1)}, u32[]{:S(2)}) %copy-start.10) | copy-done | bytes 491544
  79.6 1.6 %fusion.11 = (f32[15,4,8,4]{3,1,2,0:T(4,128)S(1)}, f32[15,4,8,4,16]{4,3,1,2,0:T(4,128)S(1)}) fusion(bf16[15,16,8,128,1]{3,2,1,0,4:T(8,128)(2,1)S(1)} %bitcast_bitcast_fusion, bf16[15,4,8,4,128]{4,3,2,1,0:T(4,128)(2,1)S(1)} %copy-done.10, pred[15,4,16]{2,1,0:T(4,128)(4,1)S(1)} %iota_compare_fusion), kind=kOutput, calls=%fused_computation.49 | convolution fusion | flops 7987215 | bytes 1114560 | tf_op jit(solution)/shard_map/sub | solution.py:407
  81.1 0.9 %fusion.5 = bf16[15,4,8,4,128]{4,3,1,2,0:T(4,128)(2,1)S(1)} fusion(f32[15,4,8,4,16]{4,3,1,2,0:T(4,128)S(1)} %get-tuple-element.27, bf16[15,16,8,128,1]{3,2,1,0,4:T(8,128)(2,1)S(1)} %bitcast_bitcast_fusion.1, f32[15,4,8,4]{3,1,2,0:T(4,128)S(1)} %get-tuple-element.26), kind=kOutput, calls=%fused_computation.7 | convolution fusion | flops 8171520 | bytes 1113600 | tf_op jit(solution)/shard_map/rtkgc,rckd->rtkgd/dot_general | solution.py:409
  82.1 0.2 copy.30
  82.3 0.9 %convert_element_type.30 = bf16[15,4,4096]{2,1,0:T(4,128)(2,1)} reshape(bf16[15,4,8,4,128]{4,3,2,1,0:T(4,128)(2,1)S(1)} %copy.30) | data formatting | bytes 983040 | tf_op jit(solution)/shard_map/convert_element_type | solution.py:412
  83.2 0.7 copy.65
  83.9 0.6 copy.66
  (39 shorter events, 1.0 us)
Async XLA Ops:
  0.6 5.0 %copy-start.7 = (bf16[15,4,4096]{2,1,0:T(4,128)(2,1)S(1)}, bf16[15,4,4096]{2,1,0:T(4,128)(2,1)}, u32[]{:S(2)}) copy-start(bf16[15,4,4096]{2,1,0:T(4,128)(2,1)} %param.19) | copy-start | bytes 1474564
  0.6 6.3 %copy-start.6 = (bf16[240,4,320]{0,2,1:T(8,128)(2,1)S(1)}, bf16[240,4,320]{0,2,1:T(8,128)(2,1)}, u32[]{:S(2)}) copy-start(bf16[240,4,320]{0,2,1:T(8,128)(2,1)} %param.12) | copy-start | bytes 1843204
  8.2 1.8 %copy-start = (bf16[2,320,1024]{2,1,0:T(8,128)(2,1)S(1)}, bf16[2,320,1024]{2,1,0:T(8,128)(2,1)}, u32[]{:S(2)}) copy-start(bf16[2,320,1024]{2,1,0:T(8,128)(2,1)} %refs_1_.1) | copy-start | bytes 3932164
  8.2 1.8 %copy-start.1 = (f32[1,2,64,320]{3,2,1,0:T(8,128)S(1)}, f32[1,2,64,320]{3,2,1,0:T(8,128)}, u32[]{:S(2)}) copy-start(f32[1,2,64,320]{3,2,1,0:T(8,128)} %param.16) | copy-start | bytes 491524
  8.2 1.8 %copy-start.2 = (f32[2,64,320]{2,1,0:T(8,128)S(1)}, f32[2,64,320]{2,1,0:T(8,128)}, u32[]{:S(2)}) copy-start(f32[2,64,320]{2,1,0:T(8,128)} %param.14) | copy-start | bytes 491524
  8.2 1.8 %copy-start.3 = (f32[1,2,64,64]{3,2,1,0:T(8,128)S(1)}, f32[1,2,64,64]{3,2,1,0:T(8,128)}, u32[]{:S(2)}) copy-start(f32[1,2,64,64]{3,2,1,0:T(8,128)} %param.17) | copy-start | bytes 98308
  8.2 1.8 %copy-start.4 = (f32[2,64,64]{2,1,0:T(8,128)S(1)}, f32[2,64,64]{2,1,0:T(8,128)}, u32[]{:S(2)}) copy-start(f32[2,64,64]{2,1,0:T(8,128)} %param.15) | copy-start | bytes 98308
  74.9 0.7 copy-start.11
  75.9 1.0 %copy-start.5 = (f32[15,4,1024]{2,1,0:T(4,128)S(1)}, f32[15,4,1024]{2,1,0:T(4,128)}, u32[]{:S(2)}) copy-start(f32[15,4,1024]{2,1,0:T(4,128)} %mul.105) | copy-start | bytes 737284
  76.8 1.0 %copy-start.8 = (bf16[15,16,1024]{2,1,0:T(8,128)(2,1)S(1)}, bf16[15,16,1024]{2,1,0:T(8,128)(2,1)}, u32[]{:S(2)}) copy-start(bf16[15,16,1024]{2,1,0:T(8,128)(2,1)} %param.21) | copy-start | bytes 1474564
  76.8 1.2 %copy-start.9 = (bf16[15,16,1024]{2,1,0:T(8,128)(2,1)S(1)}, bf16[15,16,1024]{2,1,0:T(8,128)(2,1)}, u32[]{:S(2)}) copy-start(bf16[15,16,1024]{2,1,0:T(8,128)(2,1)} %param.20) | copy-start | bytes 1474564
  78.5 1.0 %copy-start.10 = (bf16[15,4,8,4,128]{4,3,2,1,0:T(4,128)(2,1)S(1)}, bf16[15,4,8,4,128]{4,3,2,1,0:T(4,128)(2,1)}, u32[]{:S(2)}) copy-start(bf16[15,4,8,4,128]{4,3,2,1,0:T(4,128)(2,1)} %reshape.213) | copy-start | bytes 1474564

commit v2 on v1

v2 whole, which is shorter than its diff:
```python
import math

import jax
import jax.numpy as jnp
from jax import lax
from jax.experimental import pallas as pl
from jax.experimental.pallas import tpu as pltpu
from jax.sharding import PartitionSpec as P

D = 5120
KVH = 8
HD = 128
QH = 32
R = 64
STEPS = 4
KV = 2048
MESH = pl.DeviceIdType.MESH

NY = 8
NZ = 8
TOK = 64
DS = 320
NC = 4
CW = 512
HALF = CW // 2
ORDER = (4, 3, 5, 2, 6, 1, 7, 0)
GR = 384
GH = GR // 2
GZ = GH // NZ
ROWS = 15
SCALE = HD ** -0.5
NEG = -1e30
F32 = jnp.float32
BF = jnp.bfloat16


def transfer_kernel(
    rate_a, rate_b,
    hT, kv, ga, gb, fa, fb, gain, q, ck, cv, lens, pos,
    out, na, nb,
    hin, hsend, hown, hrem, wown, wrem, pk,
    sb0, rb0, sb, rb, pu, sbu, rbu,
    tpad, gT, fT, g1s, g1r, g2s, g2r, h2, g3r, tot, full, nball,
    qin, qs, qh, kc, vc, biasc, biasn, cost, sint, mc, lc, oc, pn, of,
    loc, ssem, rsem,
):
    dp = lax.axis_index("dp")
    tn = lax.axis_index("tensor")
    xh, z, c = dp // 16, lax.rem(dp // 2, 8), lax.rem(dp, 2)
    a, y = tn // NY, lax.rem(tn, NY)
    dsib = dp + 1 - 2 * c
    dflip = lax.rem(dp + 16, 32)
    tflip = lax.rem(tn + 8, 16)
    sib = (dsib, tn)
    xflip = (dflip, tn)
    part = (dp, tflip)
    other = (dflip, tflip)
    up = (dp, a * NY + lax.rem(y + 1, NY))
    down = (dp, a * NY + lax.rem(y + NY - 1, NY))
    zpeer = [None] + [(xh * 16 + lax.rem(z + i, NZ) * 2 + c, tn) for i in range(1, NZ)]
    ring = (up, down)
    peers = [sib, xflip, part, other, up, down] + zpeer[1:]

    barrier = pltpu.get_barrier_semaphore()
    for peer in peers:
        pl.semaphore_signal(barrier, inc=1, device_id=peer, device_id_type=MESH)

    def local(i, src, dst):
        cp = pltpu.make_async_copy(src, dst, loc.at[i])
        cp.start()
        return cp

    lh = [local(t, hT.at[t], hin.at[t]) for t in range(STEPS)]
    lw = []
    for k in range(NC):
        cols = pl.ds((k % 2) * CW, CW)
        lw.append(local(4 + k, kv.at[k // 2, :, cols], wown.at[k]))
    lq = local(8, q, qin)
    lk = local(9, ck, kc.at[pl.ds(0, 16 * ROWS)])
    lv = local(10, cv, vc.at[pl.ds(0, 16 * ROWS)])

    count = [0]
    started = []

    def remote(src, dst, device):
        i = count[0]
        count[0] += 1
        cp = pltpu.make_async_remote_copy(
            src_ref=src, dst_ref=dst, send_sem=ssem.at[i], recv_sem=rsem.at[i],
            device_id=device, device_id_type=MESH,
        )
        cp.start()
        started.append(cp)
        return cp

    def transposed(into, wide, narrow, by_a, by_b):
        tpad[:, 0:DS] = wide[...] * by_a
        into[...] = tpad[...].T
        tpad[:, 0:R] = narrow[...] * by_b
        into[DS:GR, :] = tpad[:, 0:128].T[0:R, :]

    tpad[...] = jnp.zeros_like(tpad)
    transposed(gT, ga, gb, -rate_a, -rate_b)

    def pick(side, into):
        row = lax.broadcasted_iota(jnp.int32, (128, 16 * ROWS), 0)
        col = lax.broadcasted_iota(jnp.int32, (128, 16 * ROWS), 1)
        target = jnp.zeros((128, 16 * ROWS), jnp.int32)
        for i, j in enumerate(ORDER):
            first = (side * NY + lax.rem(y + j, NY)) * ROWS
            target = jnp.where(row >> 4 == i, first + (row & 15), target)
        sel = jnp.where((col == target) & ((row & 15) < ROWS), 1.0, 0.0).astype(BF)
        for t in range(STEPS):
            x = lax.dot_general(
                sel, hin[t], (((1,), (1,)), ((), ())), preferred_element_type=F32
            ).astype(BF)
            for i in range(8):
                into[i * TOK + 16 * t:i * TOK + 16 * t + 16, :] = x[16 * i:16 * i + 16, :]

    for cp in lh:
        cp.wait()
    pick(1 - a, hsend)
    pl.semaphore_wait(barrier, len(peers))

    krow = c * (DS // 2)

    def weight(k, lo, n, device):
        rows = pl.ds(pl.multiple_of(krow + lo, 16), n)
        return remote(wown.at[k, rows], wrem.at[k, rows], device)

    def forward(k):
        rows = pl.ds(pl.multiple_of(krow, 16), DS // 2)
        ref = wrem.at[k, rows]
        return remote(ref, ref, sib)

    def hidden(i):
        rows = pl.ds(i * TOK, TOK)
        return remote(hsend.at[rows], hrem.at[rows], part)

    mine = pl.multiple_of(c * GH, GH)
    theirs = pl.multiple_of((1 - c) * GH, GH)
    g1s[...] = gT[pl.ds(theirs, GH), :].astype(BF)
    g1 = remote(g1s, g1r, sib)
    lw[0].wait()
    w0a = weight(0, 0, 80, part)
    w0b = weight(0, 80, 80, other)
    hr = [hidden(i) for i in range(3)]
    lw[1].wait()
    w1 = weight(1, 0, 160, other)

    def product(k, lo, n):
        pk[k, lo:lo + n, :] = jnp.dot(
            hown[lo:lo + n, :], wown[k], preferred_element_type=F32
        ) + jnp.dot(hrem[lo:lo + n, :], wrem[k], preferred_element_type=F32)

    sent = {}

    def stage(k, s):
        if s == 0:
            for way in range(2):
                cut = slice(way * HALF, way * HALF + HALF)
                sb0[k, way] = pk[k, 0:TOK, cut].astype(BF)
                sent[k, 0, way] = remote(sb0.at[k, way], rb0.at[k, way], ring[way])
            return
        for way in range(2):
            lo = (2 * s - 1 + way) * TOK
            sent[k, s - 1, way].wait_recv()
            if s == 1:
                cut = slice(way * HALF, way * HALF + HALF)
                rest = slice((1 - way) * HALF, (1 - way) * HALF + HALF)
                sb[k, 0, way, :, cut] = (
                    pk[k, lo:lo + TOK, cut] + rb0[k, way].astype(F32)
                ).astype(BF)
                sb[k, 0, way, :, rest] = pk[k, lo:lo + TOK, rest].astype(BF)
            else:
                sb[k, s - 1, way] = (
                    pk[k, lo:lo + TOK, :] + rb[k, s - 2, way].astype(F32)
                ).astype(BF)
            sent[k, s, way] = remote(sb.at[k, s - 1, way], rb.at[k, s - 1, way], ring[way])

    def last(k, u, allb):
        for way in range(2):
            sent[k, 3, way].wait_recv()
        adapter = lax.dot_general(
            u[k // 2], allb[k % 2], (((1,), (1,)), ((), ())), preferred_element_type=F32
        )
        return (
            pk[k, 7 * TOK:, :] + rb[k, 2, 0].astype(F32) + rb[k, 2, 1].astype(F32) + adapter
        )

    def prepare_masks():
        i = lax.broadcasted_iota(jnp.int32, (256, 256), 0)
        j = lax.broadcasted_iota(jnp.int32, (256, 256), 1)
        length = jnp.zeros((256, 256), jnp.int32)
        for r in range(ROWS):
            length = jnp.where(j >> 4 == r, lens[r], length)
        ok = ((i & 15) == (j >> 4)) & ((j & 15) < length)
        biasc[...] = jnp.where(ok, 0.0, NEG)
        i = lax.broadcasted_iota(jnp.int32, (256, TOK), 0)
        j = lax.broadcasted_iota(jnp.int32, (256, TOK), 1)
        ok = ((i & 15) == (j & 15)) & (((i >> 4) & 3) >= (j >> 4))
        biasn[...] = jnp.where(ok, 0.0, NEG)

    def prepare_rotation():
        row = lax.broadcasted_iota(jnp.int32, (16, HD), 0)
        place = jnp.zeros((16, HD), jnp.int32)
        for r in range(ROWS):
            place = jnp.where(row == r, pos[r], place)
        lane = lax.broadcasted_iota(jnp.int32, (16, HD), 1)
        i = lane & 63
        coarse = jnp.zeros((16, HD), F32)
        fine = jnp.zeros((16, HD), F32)
        for n in range(8):
            coarse = jnp.where(i >> 3 == n, 1000000.0 ** (-16.0 * n / HD), coarse)
            fine = jnp.where((i & 7) == n, 1000000.0 ** (-2.0 * n / HD), fine)
        freq = coarse * fine
        sign = jnp.where(lane < 64, -1.0, 1.0)
        for t in range(STEPS):
            angle = (place + t).astype(F32) * freq
            cost[16 * t:16 * t + 16, :] = jnp.cos(angle)
            sint[16 * t:16 * t + 16, :] = jnp.sin(angle) * sign

    def prepare_queries():
        lq.wait()
        qs[...] = jnp.zeros_like(qs)
        for r in range(ROWS):
            row = qin[r].astype(F32)
            for n in range(QH):
                qs[n, pl.ds(r, STEPS, stride=16), :] = row[:, n * HD:n * HD + HD]
        for h in range(KVH):
            for g in range(4):
                qh[h, g * TOK:g * TOK + TOK, :] = qs[4 * h + g].astype(BF)

    def cached(h):
        cols = slice(h * HD, h * HD + HD)
        s = lax.dot_general(
            qh[h], kc[:, cols], (((1,), (1,)), ((), ())), preferred_element_type=F32
        ) * SCALE + biasc[...]
        top = jnp.max(s, axis=-1, keepdims=True)
        e = jnp.exp(s - top)
        mc[h] = top
        lc[h] = jnp.sum(e, axis=-1, keepdims=True)
        oc[h] = jnp.dot(e.astype(BF), vc[:, cols], preferred_element_type=F32)

    def new_keys(k, x):
        for n in range(4):
            h = 4 * k + n
            v = x[:, n * HD:n * HD + HD]
            v = v * lax.rsqrt(jnp.mean(v * v, axis=-1, keepdims=True) + 1e-06) * gain[...]
            turned = jnp.concatenate([v[:, 64:], v[:, :64]], axis=-1)
            key = (v * cost[...] + turned * sint[...]).astype(BF)
            s = lax.dot_general(
                qh[h], key, (((1,), (1,)), ((), ())), preferred_element_type=F32
            ) * SCALE + biasn[...]
            top = jnp.maximum(mc[h], jnp.max(s, axis=-1, keepdims=True))
            e = jnp.exp(s - top)
            back = jnp.exp(mc[h] - top)
            inv = 1.0 / (back * lc[h] + jnp.sum(e, axis=-1, keepdims=True))
            pn[h] = (e * inv).astype(BF)
            oc[h] = oc[h] * (back * inv)

    def new_values(k, x):
        for n in range(4):
            h = 4 * (k - 2) + n
            o = oc[h] + jnp.dot(
                pn[h], x[:, n * HD:n * HD + HD].astype(BF), preferred_element_type=F32
            )
            for g in range(4):
                of[4 * h + g] = o[g * TOK:g * TOK + TOK, :]
        for r in range(ROWS):
            for n in range(16 * (k - 2), 16 * (k - 1)):
                out[r, :, n * HD:n * HD + HD] = of[n, pl.ds(r, STEPS, stride=16), :].astype(BF)

    usent = {}

    def ustage(s):
        if s == 0:
            sbu[0, 0] = pu[0:TOK, :].astype(BF)
            usent[0, 0] = remote(sbu.at[0, 0], rbu.at[0, 0], up)
            return
        for way in range(2):
            lo = (2 * s - 1 + way) * TOK
            total = pu[lo:lo + TOK, :]
            if s > 1 or way == 0:
                usent[s - 1, way].wait_recv()
                total = total + rbu[s - 1, way].astype(F32)
            sbu[s, way] = total.astype(BF)
            usent[s, way] = remote(sbu.at[s, way], rbu.at[s, way], ring[way])

    bsent = {}

    def bstage(s):
        if s > 0:
            bsent[s - 1, 0].wait_recv()
            if s < 3:
                bsent[s - 1, 1].wait_recv()
        for way in range(2 if s < 3 else 1):
            from_y = lax.rem(y + NY - s, NY) if way == 0 else lax.rem(y + s, NY)
            ref = nball.at[c, from_y]
            bsent[s, way] = remote(ref, ref, ring[way])

    prepare_masks()
    pick(a, hown)
    g1.wait_recv()
    h2[...] = gT[pl.ds(mine, GH), :] + g1r[...].astype(F32)
    g3 = []
    for i in range(1, NZ):
        rows = pl.ds(pl.multiple_of(lax.rem(z + i, NZ) * GZ, GZ), GZ)
        g3.append(remote(h2.at[rows, :], g3r.at[i], zpeer[i]))
    transposed(fT, fa, fb, 0.5, 0.5)
    prepare_queries()

    w0a.wait_recv()
    w0b.wait_recv()
    f0 = forward(0)
    hr += [hidden(i) for i in range(3, 8)]
    lw[2].wait()
    w2 = weight(2, 0, 160, other)
    hr[0].wait_recv()
    f0.wait_recv()
    product(0, 0, TOK)
    stage(0, 0)
    kc[16 * ROWS:, :] = jnp.zeros((16, 1024), BF)
    vc[16 * ROWS:, :] = jnp.zeros((16, 1024), BF)
    lk.wait()
    lv.wait()
    w1.wait_recv()
    f1 = forward(1)
    lw[3].wait()
    w3 = [weight(3, 0, 80, part), weight(3, 80, 80, other)]
    for i in (1, 2):
        hr[i].wait_recv()
    product(0, TOK, 2 * TOK)
    f1.wait_recv()
    product(1, 0, TOK)
    stage(1, 0)
    stage(0, 1)

    piece = pl.ds(pl.multiple_of(c * GH + z * GZ, GZ), GZ)
    total = h2[pl.ds(pl.multiple_of(z * GZ, GZ), GZ), :] + fT[piece, :]
    for i in range(1, NZ):
        g3[i - 1].wait_recv()
        total = total + g3r[i]
    g2s[...] = total
    g2 = [remote(g2s, g2r.at[i], device) for i, device in enumerate((xflip, part, other))]

    product(1, TOK, 2 * TOK)
    stage(1, 1)
    cached(0)
    w2.wait_recv()
    f2 = forward(2)
    for i in (3, 4):
        hr[i].wait_recv()
    product(0, 3 * TOK, 2 * TOK)
    f2.wait_recv()
    product(2, 0, TOK)
    stage(2, 0)
    stage(0, 2)

    for cp in g2:
        cp.wait_recv()
    tot[c, z, a] = total + g2r[0]
    tot[c, z, 1 - a] = g2r[1] + g2r[2]
    g4 = [remote(tot.at[c, z], tot.at[c, z], zpeer[i]) for i in range(1, NZ)]

    for cp in w3:
        cp.wait_recv()
    f3 = forward(3)
    for i in (5, 6, 7):
        hr[i].wait_recv()
    f3.wait_recv()
    product(3, 0, TOK)
    stage(3, 0)
    product(1, 3 * TOK, 5 * TOK)
    stage(1, 2)
    product(2, TOK, 7 * TOK)
    stage(2, 1)
    product(0, 5 * TOK, 3 * TOK)
    stage(0, 3)
    product(3, TOK, 7 * TOK)
    cached(1)
    stage(3, 1)

    for cp in g4:
        cp.wait_recv()
    half = tot.at[c]
    g5 = remote(half, half, sib)
    cached(2)
    g5.wait_recv()
    def new_factors(side):
        return jnp.concatenate(
            [tot[core, i, side] for core in range(2) for i in range(NZ)], axis=0
        )

    full[0] = new_factors(a)
    full[1] = new_factors(1 - a)
    for i, side in ((0, a), (1, 1 - a)):
        nball[c, y, side] = full[i, pl.ds(pl.multiple_of(DS + c * 32, 32), 32), :].astype(BF)
    bstage(0)
    pu[...] = jnp.dot(
        hown[...], full[0, 0:DS, :].astype(BF), preferred_element_type=F32
    ) + jnp.dot(hrem[...], full[1, 0:DS, :].astype(BF), preferred_element_type=F32)
    ustage(0)
    stage(1, 3)
    cached(3)
    stage(2, 2)
    bstage(1)
    ustage(1)
    cached(4)
    stage(3, 2)
    cached(5)
    bstage(2)
    ustage(2)
    stage(2, 3)
    cached(6)
    bstage(3)
    ustage(3)
    stage(3, 3)
    cached(7)
    prepare_rotation()
    back = full[0].T
    na[...] = back[:, 0:DS]
    nb[...] = back[:, DS:GR]

    bsent[3, 0].wait_recv()
    bsent[2, 1].wait_recv()
    mineb = nball.at[c]
    shared = remote(mineb, mineb, sib)
    for way in range(2):
        usent[3, way].wait_recv()
    u = (pu[7 * TOK:, :] + rbu[3, 0].astype(F32) + rbu[3, 1].astype(F32)) * 0.25
    lane = lax.broadcasted_iota(jnp.int32, u.shape, 1)
    us = [jnp.where(lane >> 6 == p, u, 0.0).astype(BF) for p in range(2)]
    shared.wait_recv()
    allb = [
        jnp.concatenate([nball[core, i, side] for i in range(NY) for core in range(2)], axis=0)
        for side in range(2)
    ]
    new_keys(0, last(0, us, allb))
    new_keys(1, last(1, us, allb))
    new_values(2, last(2, us, allb))
    new_values(3, last(3, us, allb))
    for cp in started:
        cp.wait_send()


N_REMOTE = 6 + 4 + 8 + 32 + 7 + 1 + 7 + 3 + 7 + 1 + 7 + 1


def transfers(rate_a, rate_b, *operands):
    def body(*refs):
        transfer_kernel(rate_a, rate_b, *refs)

    vmem = pl.BlockSpec(memory_space=pltpu.VMEM)
    hbm = pl.BlockSpec(memory_space=pltpu.HBM)
    smem = pl.BlockSpec(memory_space=pltpu.SMEM)
    return pl.pallas_call(
        body,
        out_shape=(
            jax.ShapeDtypeStruct((ROWS, STEPS, QH * HD), BF),
            jax.ShapeDtypeStruct((2 * R, DS), F32),
            jax.ShapeDtypeStruct((2 * R, R), F32),
        ),
        in_specs=[hbm, hbm, vmem, vmem, vmem, vmem, vmem, hbm, hbm, hbm, smem, smem],
        out_specs=(vmem, vmem, vmem),
        scratch_shapes=[
            pltpu.VMEM((STEPS, DS, 16 * ROWS), BF),
            pltpu.VMEM((8 * TOK, DS), BF),
            pltpu.VMEM((8 * TOK, DS), BF),
            pltpu.VMEM((8 * TOK, DS), BF),
            pltpu.VMEM((NC, DS, CW), BF),
            pltpu.VMEM((NC, DS, CW), BF),
            pltpu.VMEM((NC, 8 * TOK, CW), F32),
            pltpu.VMEM((NC, 2, TOK, HALF), BF),
            pltpu.VMEM((NC, 2, TOK, HALF), BF),
            pltpu.VMEM((NC, 3, 2, TOK, CW), BF),
            pltpu.VMEM((NC, 3, 2, TOK, CW), BF),
            pltpu.VMEM((8 * TOK, 128), F32),
            pltpu.VMEM((4, 2, TOK, 128), BF),
            pltpu.VMEM((4, 2, TOK, 128), BF),
            pltpu.VMEM((128, GR), F32),
            pltpu.VMEM((GR, 128), F32),
            pltpu.VMEM((GR, 128), F32),
            pltpu.VMEM((GH, 128), BF),
            pltpu.VMEM((GH, 128), BF),
            pltpu.VMEM((GZ, 128), F32),
            pltpu.VMEM((3, GZ, 128), F32),
            pltpu.VMEM((GH, 128), F32),
            pltpu.VMEM((NZ, GZ, 128), F32),
            pltpu.VMEM((2, NZ, 2, GZ, 128), F32),
            pltpu.VMEM((2, GR, 128), F32),
            pltpu.VMEM((2, NY, 2, 32, 128), BF),
            pltpu.VMEM((ROWS, STEPS, QH * HD), BF),
            pltpu.VMEM((QH, TOK, HD), F32),
            pltpu.VMEM((KVH, 256, HD), BF),
            pltpu.VMEM((256, 1024), BF),
            pltpu.VMEM((256, 1024), BF),
            pltpu.VMEM((256, 256), F32),
            pltpu.VMEM((256, TOK), F32),
            pltpu.VMEM((TOK, HD), F32),
            pltpu.VMEM((TOK, HD), F32),
            pltpu.VMEM((KVH, 256, 1), F32),
            pltpu.VMEM((KVH, 256, 1), F32),
            pltpu.VMEM((KVH, 256, HD), F32),
            pltpu.VMEM((KVH, 256, TOK), BF),
            pltpu.VMEM((QH, TOK, HD), F32),
            pltpu.SemaphoreType.DMA((11,)),
            pltpu.SemaphoreType.DMA((N_REMOTE,)),
            pltpu.SemaphoreType.DMA((N_REMOTE,)),
        ],
        compiler_params=pltpu.CompilerParams(
            collective_id=0, has_side_effects=True, vmem_limit_bytes=56 * 1024 * 1024
        ),
    )(*operands)


def per_device(
    hidden_in, kv_weight, factor_a, factor_b, grad_a, grad_b, key_gain,
    queries, cache_keys, cache_values, cache_lengths, positions,
):
    groups_dp = lax.axis_size("dp")
    rate_a = 2.0 / math.sqrt(groups_dp * D)
    rate_b = 2.0 / math.sqrt(groups_dp * R)
    attended, na, nb = transfers(
        rate_a, rate_b, hidden_in.transpose(1, 2, 0), kv_weight,
        grad_a.reshape(2 * R, DS), grad_b.reshape(2 * R, R),
        factor_a.reshape(2 * R, DS), factor_b.reshape(2 * R, R),
        key_gain.reshape(1, HD), queries,
        cache_keys.reshape(16 * ROWS, KVH * HD), cache_values.reshape(16 * ROWS, KVH * HD),
        cache_lengths, positions,
    )
    return (attended, na.reshape(2, R, DS), nb.reshape(2, R, R))


def solution(mesh):
    return jax.shard_map(
        per_device,
        mesh=mesh,
        in_specs=(
            P("dp", None, "tensor"),
            P(None, "tensor", None),
            P(None, None, "tensor"),
            P(None, None, "tensor"),
            P("dp", None, None, "tensor"),
            P("dp", None, None, "tensor"),
            P(),
            P(("dp", "tensor"), None, None),
            P(("dp", "tensor"), None, None),
            P(("dp", "tensor"), None, None),
            P(("dp", "tensor")),
            P(("dp", "tensor")),
        ),
        out_specs=(
            P(("dp", "tensor"), None, None),
            P(None, None, "tensor"),
            P(None, None, "tensor"),
        ),
        check_vma=False,
    )
```

time: 84.8 us -> 63.5 us (0.75)
  local copies, waits for them, and re-layouts: 11.5 us -> 4.29 us
  Pallas kernels: 64.9 us -> 58.4 us
  other arithmetic: 4.68 us -> 0 us
  matrix products: 2.5 us -> 0 us
    pallas_call x1, Pallas kernels: 64.9 us -> 58.4 us  [transfers(): pl.pallas_call(body, out_shape=(jax.ShapeDtypeStruct((ROWS, STEPS, QH * H...]
    reshape x7 -> x0, local copies, waits for them, and re-layouts: 3.54 us -> none  [the longest x1 1.67 us: per_device(): hidden_in.reshape(16, rows_here * STEPS, DS)]
    mul x6 -> x0, local copies, waits for them, and re-layouts: 1.74 us -> none  [the longest x3 0.88 us: normed_rotated(): return keys * cosine + turned * sine]
    sub x1 -> x0, matrix products: 1.56 us -> none  [attend(): expo = jnp.exp(scores - top)]
    add x2 -> x0, other arithmetic: 1.48 us -> none  [the longest x1 0.75 us: attend(): hit = (slot[None, :] == lengths[:, None] + step)[:, :, None]]
    convert_element_type x2 -> x0, local copies, waits for them, and re-layouts: 1.1 us -> none  [attend(): return result.reshape(rows, steps, width).astype(jnp.bfloat16)]
    dot_general x1 -> x0, matrix products: 0.93 us -> none  [attend(): jnp.einsum('rtkgc,rckd->rtkgd', weights, value_four, preferred_element_ty...]
    convert_element_type x2 -> x0, other arithmetic: 0.89 us -> none  [the longest x1 0.73 us: normed_rotated(): angle = position.astype(jnp.float32)[..., None] * freq]
where the time goes in v2:
time: 63.5 us; the launch traced here: 63.3 us
  Pallas kernels  58.4 us (92%)
  local copies, waits for them, and re-layouts  4.29 us (7%)
  between operations  0.65 us (1%)
    pallas_call x1, Pallas kernels, transfers(): pl.pallas_call(body, out_shape=(jax.ShapeDtypeStruct((ROWS, STEPS, QH * H...  58.4 us
    unnamed x5, local copies, waits for them, and re-layouts  4.29 us

profile of v2, /device:TPU:1, one launch (start us, length us, event | category | flops | bytes accessed | tf_op | source)
XLA Modules:
  0.0 63.3 jit_solution(17759026861733802644)
XLA Ops:
  0.6 58.4 %shard_map.139 = (bf16[15,4,4096]{2,1,0:T(4,128)(2,1)}, f32[128,320]{1,0:T(8,128)}, f32[128,64]{1,0:T(8,128)}) custom-call(bf16[4,320,240]{2,1,0:T(8,128)(2,1)} %bitcast.10, bf16[2,320,1024]{2,1,0:T(8,128)(2,1)} %refs_1_.1, f32[128,320]{1,0:T(8,128)} %bitcast.13, f32[128,64]{1,0:T(8,128)} %bitcast.16, f32[128,320]{1,0:T(8,128)} %bitcast.14, ...), custom_call_target="tpu_custom_call" | custom-call | tf_op jit(solution)/shard_map/pallas_call | solution.py:457
  59.0 0.0 copy-start
  59.0 2.0 %copy.18 = bf16[15,4,4096]{2,1,0:T(4,128)(2,1)} copy(bf16[15,4,4096]{2,1,0:T(4,128)(2,1)} %get-tuple-element.12) | data formatting | bytes 983040
  61.1 1.6 %copy.19 = f32[2,64,320]{2,1,0:T(8,128)} copy(f32[2,64,320]{2,1,0:T(8,128)} %bitcast.15) | data formatting | bytes 327680
  62.7 0.0 copy-done
  62.7 0.6 copy.20
Async XLA Ops:
  59.0 3.7 %copy-start = (f32[128,64]{1,0:T(8,128)S(1)}, f32[128,64]{1,0:T(8,128)}, u32[]{:S(2)}) copy-start(f32[128,64]{1,0:T(8,128)} %get-tuple-element.8) | copy-start | bytes 98308

commit v3 on v2

v3 whole, which is shorter than its diff:
```python
import math

import jax
import jax.numpy as jnp
from jax import lax
from jax.experimental import pallas as pl
from jax.experimental.pallas import tpu as pltpu
from jax.sharding import PartitionSpec as P

D = 5120
KVH = 8
HD = 128
QH = 32
R = 64
STEPS = 4
KV = 2048
MESH = pl.DeviceIdType.MESH

NY = 8
NZ = 8
TOK = 64
DS = 320
ORDER = (4, 3, 5, 2, 6, 1, 7, 0)
NC = 5
WIDTH = (512, 256, 512, 512, 512)
PIECES = ((0,), (1,), (2, 3), (4, 5), (6, 7))
GR = 384
GP = 512
GH = GP // 2
GZ = GH // NZ
ROWS = 15
SCALE = HD ** -0.5
NEG = -1e30
F32 = jnp.float32
BF = jnp.bfloat16


def transfer_kernel(
    rate_a, rate_b,
    hT, kv, ga, gb, fa, fb, gain, q, ck, cv, lens, pos,
    out, na, nb,
    hin, hsend, hown, hrem, wfirst, wown, wrem, wnarrow, wnarrowr,
    pk, pknarrow, sb0, rb0, sb, rb, sb0l, rb0l, sbl, rbl, first, xs, xr,
    pu, sbu, rbu,
    gav, gbv, fav, fbv, tpad, gT, fT, g1s, g1r, h2, g3r, g2s, g2r, tot, nball, hball, b3r, b2s, b2r,
    qin, qs, qh, kc, vc, biasc, biasn, cost, sint, mc, lc, oc, pn, of, outv, nav, nbv,
    loc, ssem, rsem,
):
    dp = lax.axis_index("dp")
    tn = lax.axis_index("tensor")
    xh, z, c = dp // 16, lax.rem(dp // 2, 8), lax.rem(dp, 2)
    a, y = tn // NY, lax.rem(tn, NY)
    dflip = lax.rem(dp + 16, 32)
    tflip = lax.rem(tn + 8, 16)
    sib = (dp + 1 - 2 * c, tn)
    xflip = (dflip, tn)
    part = (dp, tflip)
    other = (dflip, tflip)
    ypeer = [None] + [(dp, a * NY + lax.rem(y + i, NY)) for i in range(1, NY)]
    zpeer = [None] + [(xh * 16 + lax.rem(z + i, NZ) * 2 + c, tn) for i in range(1, NZ)]
    ring = (ypeer[1], ypeer[NY - 1])
    peers = [sib, xflip, part, other] + ypeer[1:] + zpeer[1:]

    barrier = pltpu.get_barrier_semaphore()
    for peer in peers:
        pl.semaphore_signal(barrier, inc=1, device_id=peer, device_id_type=MESH)

    nloc = [0]

    def local(src, dst):
        cp = pltpu.make_async_copy(src, dst, loc.at[nloc[0]])
        nloc[0] += 1
        cp.start()
        return cp

    lh = [local(hT.at[t], hin.at[t]) for t in range(STEPS)]
    lw = [local(kv.at[0, :, pl.ds(0, 256)], wfirst), local(kv.at[0, :, pl.ds(256, 256)], wnarrow)]
    lg = [local(ga, gav), local(gb, gbv)]
    lw += [
        local(kv.at[0, :, pl.ds(512, 512)], wown.at[0]),
        local(kv.at[1, :, pl.ds(0, 512)], wown.at[1]),
        local(kv.at[1, :, pl.ds(512, 512)], wown.at[2]),
    ]
    lq = local(q, qin)
    lk = local(ck, kc.at[pl.ds(0, 16 * ROWS)])
    lv = local(cv, vc.at[pl.ds(0, 16 * ROWS)])
    lf = [local(fa, fav), local(fb, fbv)]

    count = [0]
    started = []

    def remote(src, dst, device):
        i = count[0]
        count[0] += 1
        cp = pltpu.make_async_remote_copy(
            src_ref=src, dst_ref=dst, send_sem=ssem.at[i], recv_sem=rsem.at[i],
            device_id=device, device_id_type=MESH,
        )
        cp.start()
        started.append(cp)
        return cp

    def transposed(into, wide, narrow, by_a, by_b):
        tpad[:, 0:DS] = wide[...] * by_a
        into[0:GR, :] = tpad[...].T
        tpad[:, 0:R] = narrow[...] * by_b
        into[DS:GR, :] = tpad[:, 0:128].T[0:R, :]

    def pick(side, into):
        row = lax.broadcasted_iota(jnp.int32, (128, 16 * ROWS), 0)
        col = lax.broadcasted_iota(jnp.int32, (128, 16 * ROWS), 1)
        target = jnp.zeros((128, 16 * ROWS), jnp.int32)
        for i, j in enumerate(ORDER):
            first = (side * NY + lax.rem(y + j, NY)) * ROWS
            target = jnp.where(row >> 4 == i, first + (row & 15), target)
        sel = jnp.where((col == target) & ((row & 15) < ROWS), 1.0, 0.0).astype(BF)
        for t in range(STEPS):
            x = lax.dot_general(
                sel, hin[t], (((1,), (1,)), ((), ())), preferred_element_type=F32
            ).astype(BF)
            for i in range(8):
                into[i * TOK + 16 * t:i * TOK + 16 * t + 16, :] = x[16 * i:16 * i + 16, :]

    wo = (None, wnarrow, wown.at[0], wown.at[1], wown.at[2])
    wr = (None, wnarrowr, wrem.at[0], wrem.at[1], wrem.at[2])
    krow = c * (DS // 2)

    def weight(k, lo, n, device):
        rows = pl.ds(pl.multiple_of(krow + lo, 16), n)
        return remote(wo[k].at[rows], wr[k].at[rows], device)

    def forward(k):
        ref = wr[k].at[pl.ds(pl.multiple_of(krow, 16), DS // 2)]
        return remote(ref, ref, sib)

    def hidden(i):
        rows = pl.ds(i * TOK, TOK)
        return remote(hsend.at[rows], hrem.at[rows], part)

    pks = [pk.at[0], pknarrow, pk.at[1], pk.at[2], pk.at[3]]

    def product(k, lo, n):
        rows = slice(lo, lo + n)
        if k == 0:
            pk[0, rows, 0:256] = jnp.dot(hown[rows, :], wfirst[...], preferred_element_type=F32)
            pk[0, rows, 256:512] = jnp.dot(hsend[rows, :], wfirst[...], preferred_element_type=F32)
            return
        pks[k][rows, :] = jnp.dot(
            hown[rows, :], wo[k][...], preferred_element_type=F32
        ) + jnp.dot(hrem[rows, :], wr[k][...], preferred_element_type=F32)

    def slot(k, s, way):
        n = max(k - 1, 0)
        if s == 0:
            return (sb0l.at[way], rb0l.at[way]) if k == 1 else (sb0.at[n, way], rb0.at[n, way])
        if k == 1:
            return sbl.at[s - 1, way], rbl.at[s - 1, way]
        return sb.at[n, s - 1, way], rb.at[n, s - 1, way]

    sent = {}

    def stage(k, s):
        half = WIDTH[k] // 2
        for way in range(2):
            src, dst = slot(k, s, way)
            cut = slice(way * half, way * half + half)
            rest = slice((1 - way) * half, (1 - way) * half + half)
            if s == 0:
                src[...] = pks[k][0:TOK, cut].astype(BF)
            else:
                rows = slice((2 * s - 1 + way) * TOK, (2 * s + way) * TOK)
                sent[k, s - 1, way].wait_recv()
                got = slot(k, s - 1, way)[1]
                if s == 1:
                    src[:, cut] = (pks[k][rows, cut] + got[...].astype(F32)).astype(BF)
                    src[:, rest] = pks[k][rows, rest].astype(BF)
                else:
                    src[...] = (pks[k][rows, :] + got[...].astype(F32)).astype(BF)
            sent[k, s, way] = remote(src, dst, ring[way])

    def last(k):
        total = pks[k][7 * TOK:8 * TOK, :]
        for way in range(2):
            sent[k, 3, way].wait_recv()
            total = total + slot(k, 3, way)[1][...].astype(F32)
        return total

    def adapter(j):
        return lax.dot_general(
            us[j // 4], allb[(j % 4) // 2][(j % 2) * 256:(j % 2) * 256 + 256],
            (((1,), (1,)), ((), ())), preferred_element_type=F32,
        )

    def prepare_masks():
        j = lax.broadcasted_iota(jnp.int32, (256, 256), 0)
        i = lax.broadcasted_iota(jnp.int32, (256, 256), 1)
        length = jnp.zeros((256, 256), jnp.int32)
        for r in range(ROWS):
            length = jnp.where(j >> 4 == r, lens[r], length)
        ok = ((i & 15) == (j >> 4)) & ((j & 15) < length)
        biasc[...] = jnp.where(ok, 0.0, NEG)
        j = lax.broadcasted_iota(jnp.int32, (TOK, 256), 0)
        i = lax.broadcasted_iota(jnp.int32, (TOK, 256), 1)
        ok = ((i & 15) == (j & 15)) & (((i >> 4) & 3) >= (j >> 4))
        biasn[...] = jnp.where(ok, 0.0, NEG)

    def prepare_rotation():
        row = lax.broadcasted_iota(jnp.int32, (16, HD), 0)
        place = jnp.zeros((16, HD), jnp.int32)
        for r in range(ROWS):
            place = jnp.where(row == r, pos[r], place)
        lane = lax.broadcasted_iota(jnp.int32, (16, HD), 1)
        i = lane & 63
        coarse = jnp.zeros((16, HD), F32)
        fine = jnp.zeros((16, HD), F32)
        for n in range(8):
            coarse = jnp.where(i >> 3 == n, 1000000.0 ** (-16.0 * n / HD), coarse)
            fine = jnp.where((i & 7) == n, 1000000.0 ** (-2.0 * n / HD), fine)
        freq = coarse * fine
        sign = jnp.where(lane < 64, -1.0, 1.0)
        for t in range(STEPS):
            angle = (place + t).astype(F32) * freq
            cost[16 * t:16 * t + 16, :] = jnp.cos(angle)
            sint[16 * t:16 * t + 16, :] = jnp.sin(angle) * sign

    def prepare_queries():
        lq.wait()
        qs[...] = jnp.zeros_like(qs)
        for r in range(ROWS):
            row = qin[r].astype(F32)
            for n in range(QH):
                qs[n, pl.ds(r, STEPS, stride=16), :] = row[:, n * HD:n * HD + HD]
        for h in range(KVH):
            for g in range(4):
                qh[h, g * TOK:g * TOK + TOK, :] = qs[4 * h + g].astype(BF)

    def cached(h):
        cols = slice(h * HD, h * HD + HD)
        s = lax.dot_general(
            kc[:, cols], qh[h], (((1,), (1,)), ((), ())), preferred_element_type=F32
        ) * SCALE + biasc[...]
        top = jnp.max(s, axis=0, keepdims=True)
        e = jnp.exp(s - top)
        mc[h] = top
        lc[h] = jnp.sum(e, axis=0, keepdims=True)
        oc[h] = lax.dot_general(
            vc[:, cols], e.astype(BF), (((0,), (0,)), ((), ())), preferred_element_type=F32
        )

    def new_keys(j, x):
        for n in range(2):
            h = 2 * j + n
            v = x[:, n * HD:n * HD + HD]
            v = v * lax.rsqrt(jnp.mean(v * v, axis=-1, keepdims=True) + 1e-06) * gain[...]
            turned = jnp.concatenate([v[:, 64:], v[:, :64]], axis=-1)
            key = (v * cost[...] + turned * sint[...]).astype(BF)
            s = lax.dot_general(
                key, qh[h], (((1,), (1,)), ((), ())), preferred_element_type=F32
            ) * SCALE + biasn[...]
            top = jnp.maximum(mc[h], jnp.max(s, axis=0, keepdims=True))
            e = jnp.exp(s - top)
            back = jnp.exp(mc[h] - top)
            inv = 1.0 / (back * lc[h] + jnp.sum(e, axis=0, keepdims=True))
            pn[h] = (e * inv).astype(BF)
            oc[h] = oc[h] * (back * inv)

    lo_ = []

    def new_values(j, x):
        for n in range(2):
            h = 2 * (j - 4) + n
            o = oc[h] + lax.dot_general(
                x[:, n * HD:n * HD + HD].astype(BF), pn[h], (((0,), (0,)), ((), ())),
                preferred_element_type=F32,
            )
            o = o.T
            for g in range(4):
                of[4 * h + g] = o[g * TOK:g * TOK + TOK, :]
        for r in range(ROWS):
            for n in range(8 * (j - 4), 8 * (j - 3)):
                outv[r, :, n * HD:n * HD + HD] = of[n, pl.ds(r, STEPS, stride=16), :].astype(BF)
        cols = pl.ds((j - 4) * 1024, 1024)
        lo_.append(local(outv.at[:, :, cols], out.at[:, :, cols]))

    tpad[...] = jnp.zeros_like(tpad)
    gT[GR:, :] = jnp.zeros((GP - GR, 128), F32)
    mine = pl.multiple_of(c * GH, GH)
    theirs = pl.multiple_of((1 - c) * GH, GH)
    for cp in lg:
        cp.wait()
    transposed(gT, gav, gbv, -rate_a, -rate_b)
    g1s[0:GH, :] = gT[pl.ds(theirs, GH), :].astype(BF)
    bmine = pl.ds(pl.multiple_of(DS + c * 32, 32), 32)
    btheirs = pl.ds(pl.multiple_of(DS + (1 - c) * 32, 32), 32)
    g1s[GH:, :] = gT[btheirs, :].astype(BF)
    for cp in lh:
        cp.wait()
    pick(a, hown)
    pick(1 - a, hsend)
    lw[0].wait()
    product(0, 0, TOK)
    pl.semaphore_wait(barrier, len(peers))

    g1 = remote(g1s, g1r, sib)
    stage(0, 0)
    lw[1].wait()
    w1 = [weight(1, 0, 80, part), weight(1, 80, 80, other)]
    hr = [hidden(0)]
    lw[2].wait()
    w2 = weight(2, 0, 160, other)
    hr += [hidden(i) for i in range(1, 5)]

    g1.wait_recv()
    h2[...] = (gT[pl.ds(mine, GH), :] + g1r[0:GH, :].astype(F32)).astype(BF)
    g3 = []
    for i in range(1, NZ):
        rows = pl.ds(pl.multiple_of(lax.rem(z + i, NZ) * GZ, GZ), GZ)
        g3.append(remote(h2.at[rows, :], g3r.at[i], zpeer[i]))
    product(0, TOK, 7 * TOK)
    for cp in lf:
        cp.wait()
    fT[GR:, :] = jnp.zeros((GP - GR, 128), F32)
    transposed(fT, fav, fbv, 0.5, 0.5)
    hball[y] = (
        gT[bmine, :] + g1r[GH:, :].astype(F32) + fT[bmine, :] * 0.125
    ).astype(BF)
    b0 = [remote(hball.at[y], hball.at[y], ypeer[i]) for i in range(1, NY)]
    stage(0, 1)

    for cp in w1:
        cp.wait_recv()
    f1 = forward(1)
    lw[3].wait()
    w3 = weight(3, 0, 160, other)
    lw[4].wait()
    w4 = [weight(4, 0, 80, part)]
    hr += [hidden(i) for i in range(5, 8)]
    w4.append(weight(4, 80, 80, other))
    prepare_masks()
    hr[0].wait_recv()
    f1.wait_recv()
    product(1, 0, TOK)
    stage(1, 0)
    for i in (1, 2):
        hr[i].wait_recv()
    product(1, TOK, 2 * TOK)
    w2.wait_recv()
    f2 = forward(2)
    stage(0, 2)

    piece = pl.ds(pl.multiple_of(c * GH + z * GZ, GZ), GZ)
    total = h2[pl.ds(pl.multiple_of(z * GZ, GZ), GZ), :].astype(F32) + fT[piece, :]
    for i in range(1, NZ):
        g3[i - 1].wait_recv()
        total = total + g3r[i].astype(F32)
    g2s[...] = total
    g2 = [remote(g2s, g2r.at[i], device) for i, device in enumerate((xflip, part, other))]
    for cp in b0:
        cp.wait_recv()
    b3 = [
        remote(hball.at[lax.rem(z + i, NZ)], b3r.at[i], zpeer[i]) for i in range(1, NZ)
    ]

    f2.wait_recv()
    product(2, 0, TOK)
    stage(2, 0)
    stage(1, 1)
    prepare_queries()
    kc[16 * ROWS:, :] = jnp.zeros((16, 1024), BF)
    vc[16 * ROWS:, :] = jnp.zeros((16, 1024), BF)
    for i in (3, 4):
        hr[i].wait_recv()
    product(2, TOK, 4 * TOK)
    w3.wait_recv()
    f3 = forward(3)
    stage(0, 3)
    product(1, 3 * TOK, 2 * TOK)
    f3.wait_recv()
    product(3, 0, TOK)
    stage(3, 0)

    for cp in g2:
        cp.wait_recv()
    tot[c, z, a] = (g2s[...] + g2r[0]).astype(BF)
    tot[c, z, 1 - a] = (g2r[1] + g2r[2]).astype(BF)
    g4 = [remote(tot.at[c, z], tot.at[c, z], zpeer[i]) for i in range(1, NZ)]

    stage(2, 1)
    stage(1, 2)
    for cp in w4:
        cp.wait_recv()
    f4 = forward(4)
    lk.wait()
    lv.wait()
    total = last(0)
    xs[...] = total[:, 256:512].astype(BF)
    x0 = remote(xs, xr, part)
    first[...] = total[:, 0:256]
    total = hball[z].astype(F32)
    for i in range(1, NZ):
        b3[i - 1].wait_recv()
        total = total + b3r[i].astype(F32)
    b2s[...] = total
    b2 = [remote(b2s, b2r.at[i], device) for i, device in enumerate((xflip, part, other))]
    product(3, TOK, 4 * TOK)
    f4.wait_recv()
    product(4, 0, TOK)
    stage(4, 0)
    stage(3, 1)
    for cp in g4:
        cp.wait_recv()
    g5 = remote(tot.at[c], tot.at[c], sib)
    for i in (5, 6, 7):
        hr[i].wait_recv()
    product(2, 5 * TOK, 3 * TOK)
    stage(2, 2)
    g5.wait_recv()

    def new_a(side):
        return jnp.concatenate([tot[e // NZ, e % NZ, side] for e in range(10)], axis=0)

    pu[...] = jnp.dot(hown[...], new_a(a), preferred_element_type=F32) + jnp.dot(
        hrem[...], new_a(1 - a), preferred_element_type=F32
    )
    u1 = []
    for i in range(7):
        sbu[i] = pu[i * TOK:(i + 1) * TOK, :].astype(BF)
        u1.append(remote(sbu.at[i], rbu.at[i], ypeer[ORDER[i]]))
    for cp in b2:
        cp.wait_recv()
    nball[c, z, a] = (b2s[...] + b2r[0]).astype(BF)
    nball[c, z, 1 - a] = (b2r[1] + b2r[2]).astype(BF)
    b4 = [remote(nball.at[c, z], nball.at[c, z], zpeer[i]) for i in range(1, NZ)]
    product(1, 5 * TOK, 3 * TOK)
    stage(1, 3)
    product(4, TOK, 7 * TOK)
    stage(4, 1)
    product(3, 5 * TOK, 3 * TOK)
    stage(3, 2)
    cached(0)
    stage(2, 3)
    cached(1)

    stage(4, 2)
    stage(3, 3)
    for cp in b4:
        cp.wait_recv()
    b5 = remote(nball.at[c], nball.at[c], sib)
    cached(2)
    stage(4, 3)
    cached(3)
    for h in range(4, KVH):
        cached(h)
    prepare_rotation()
    back = jnp.concatenate([tot[e // NZ, e % NZ, a].astype(F32) for e in range(12)], axis=0).T
    nav[...] = back[:, 0:DS]
    lo_ += [local(nav, na)]

    u = pu[7 * TOK:, :]
    for i in range(7):
        u1[i].wait_recv()
        u = u + rbu[i].astype(F32)
    u = u * 0.25
    lane = lax.broadcasted_iota(jnp.int32, u.shape, 1)
    us = [jnp.where(lane >> 6 == p, u, 0.0).astype(BF) for p in range(2)]
    x0.wait_recv()
    b5.wait_recv()
    back = jnp.concatenate(
        [nball[0, y, a].astype(F32), nball[1, y, a].astype(F32), jnp.zeros((64, 128), F32)], axis=0
    ).T
    nbv[...] = back[:, 0:R]
    lo_ += [local(nbv, nb)]
    allb = [
        jnp.concatenate([nball[core, i, side] for i in range(NY) for core in range(2)], axis=0)
        for side in range(2)
    ]
    new_keys(0, first[...] + xr[...].astype(F32) + adapter(0))
    for k in range(1, NC):
        total = last(k)
        for n, j in enumerate(PIECES[k]):
            x = total[:, n * 256:n * 256 + 256] + adapter(j)
            if j < 4:
                new_keys(j, x)
            else:
                new_values(j, x)
    assert count[0] == N_REMOTE and nloc[0] == N_LOCAL
    for cp in lo_:
        cp.wait()
    for cp in started:
        cp.wait_send()


N_LOCAL = 22
N_REMOTE = 6 + 4 + 8 + 40 + 7 + 1 + 7 + 3 + 7 + 1 + 1 + 7 + 7 + 3 + 7 + 1


def transfers(rate_a, rate_b, *operands):
    def body(*refs):
        transfer_kernel(rate_a, rate_b, *refs)

    vmem = pl.BlockSpec(memory_space=pltpu.VMEM)
    hbm = pl.BlockSpec(memory_space=pltpu.HBM)
    smem = pl.BlockSpec(memory_space=pltpu.SMEM)
    return pl.pallas_call(
        body,
        out_shape=(
            jax.ShapeDtypeStruct((ROWS, STEPS, QH * HD), BF),
            jax.ShapeDtypeStruct((2 * R, DS), F32),
            jax.ShapeDtypeStruct((2 * R, R), F32),
        ),
        in_specs=[hbm] * 6 + [vmem, hbm, hbm, hbm, smem, smem],
        out_specs=(hbm, hbm, hbm),
        scratch_shapes=[
            pltpu.VMEM((STEPS, DS, 16 * ROWS), BF),
            pltpu.VMEM((8 * TOK, DS), BF),
            pltpu.VMEM((8 * TOK, DS), BF),
            pltpu.VMEM((8 * TOK, DS), BF),
            pltpu.VMEM((DS, 256), BF),
            pltpu.VMEM((3, DS, 512), BF),
            pltpu.VMEM((3, DS, 512), BF),
            pltpu.VMEM((DS, 256), BF),
            pltpu.VMEM((DS, 256), BF),
            pltpu.VMEM((4, 8 * TOK, 512), F32),
            pltpu.VMEM((8 * TOK, 256), F32),
            pltpu.VMEM((4, 2, TOK, 256), BF),
            pltpu.VMEM((4, 2, TOK, 256), BF),
            pltpu.VMEM((4, 3, 2, TOK, 512), BF),
            pltpu.VMEM((4, 3, 2, TOK, 512), BF),
            pltpu.VMEM((2, TOK, 128), BF),
            pltpu.VMEM((2, TOK, 128), BF),
            pltpu.VMEM((3, 2, TOK, 256), BF),
            pltpu.VMEM((3, 2, TOK, 256), BF),
            pltpu.VMEM((TOK, 256), F32),
            pltpu.VMEM((TOK, 256), BF),
            pltpu.VMEM((TOK, 256), BF),
            pltpu.VMEM((8 * TOK, 128), F32),
            pltpu.VMEM((7, TOK, 128), BF),
            pltpu.VMEM((7, TOK, 128), BF),
            pltpu.VMEM((2 * R, DS), F32),
            pltpu.VMEM((2 * R, R), F32),
            pltpu.VMEM((2 * R, DS), F32),
            pltpu.VMEM((2 * R, R), F32),
            pltpu.VMEM((128, GR), F32),
            pltpu.VMEM((GP, 128), F32),
            pltpu.VMEM((GP, 128), F32),
            pltpu.VMEM((GH + 32, 128), BF),
            pltpu.VMEM((GH + 32, 128), BF),
            pltpu.VMEM((GH, 128), BF),
            pltpu.VMEM((NZ, GZ, 128), BF),
            pltpu.VMEM((GZ, 128), F32),
            pltpu.VMEM((3, GZ, 128), F32),
            pltpu.VMEM((2, NZ, 2, GZ, 128), BF),
            pltpu.VMEM((2, NY, 2, 32, 128), BF),
            pltpu.VMEM((NY, 32, 128), BF),
            pltpu.VMEM((NZ, 32, 128), BF),
            pltpu.VMEM((32, 128), F32),
            pltpu.VMEM((3, 32, 128), F32),
            pltpu.VMEM((ROWS, STEPS, QH * HD), BF),
            pltpu.VMEM((QH, TOK, HD), F32),
            pltpu.VMEM((KVH, 256, HD), BF),
            pltpu.VMEM((256, 1024), BF),
            pltpu.VMEM((256, 1024), BF),
            pltpu.VMEM((256, 256), F32),
            pltpu.VMEM((TOK, 256), F32),
            pltpu.VMEM((TOK, HD), F32),
            pltpu.VMEM((TOK, HD), F32),
            pltpu.VMEM((KVH, 1, 256), F32),
            pltpu.VMEM((KVH, 1, 256), F32),
            pltpu.VMEM((KVH, HD, 256), F32),
            pltpu.VMEM((KVH, TOK, 256), BF),
            pltpu.VMEM((QH, TOK, HD), F32),
            pltpu.VMEM((ROWS, STEPS, QH * HD), BF),
            pltpu.VMEM((2 * R, DS), F32),
            pltpu.VMEM((2 * R, R), F32),
            pltpu.SemaphoreType.DMA((N_LOCAL,)),
            pltpu.SemaphoreType.DMA((N_REMOTE,)),
            pltpu.SemaphoreType.DMA((N_REMOTE,)),
        ],
        compiler_params=pltpu.CompilerParams(
            collective_id=0, has_side_effects=True, vmem_limit_bytes=56 * 1024 * 1024
        ),
    )(*operands)


def results_kernel(att, na, nb, att_out, na_out, nb_out, attv, nav, nbv, sem):
    parts = [(att.at[pl.ds(3 * i, 3)], attv.at[pl.ds(3 * i, 3)], att_out.at[pl.ds(3 * i, 3)])
             for i in range(5)]
    parts += [(na, nav, na_out), (nb, nbv, nb_out)]
    reads = [pltpu.make_async_copy(x, v, sem.at[0, i]) for i, (x, v, _) in enumerate(parts)]
    writes = [pltpu.make_async_copy(v, o, sem.at[1, i]) for i, (_, v, o) in enumerate(parts)]
    for cp in reads:
        cp.start()
    for read, write in zip(reads, writes):
        read.wait()
        write.start()
    for cp in writes:
        cp.wait()


def results(*operands):
    hbm = pl.BlockSpec(memory_space=pltpu.HBM)
    return pl.pallas_call(
        results_kernel,
        out_shape=tuple(jax.ShapeDtypeStruct(x.shape, x.dtype) for x in operands),
        in_specs=[hbm] * 3,
        out_specs=(hbm,) * 3,
        scratch_shapes=[pltpu.VMEM(x.shape, x.dtype) for x in operands]
        + [pltpu.SemaphoreType.DMA((2, 7))],
        compiler_params=pltpu.CompilerParams(vmem_limit_bytes=56 * 1024 * 1024),
    )(*operands)


def per_device(
    hidden_in, kv_weight, factor_a, factor_b, grad_a, grad_b, key_gain,
    queries, cache_keys, cache_values, cache_lengths, positions,
):
    groups_dp = lax.axis_size("dp")
    rate_a = 2.0 / math.sqrt(groups_dp * D)
    rate_b = 2.0 / math.sqrt(groups_dp * R)
    attended, na, nb = results(*transfers(
        rate_a, rate_b, hidden_in.transpose(1, 2, 0), kv_weight,
        grad_a.reshape(2 * R, DS), grad_b.reshape(2 * R, R),
        factor_a.reshape(2 * R, DS), factor_b.reshape(2 * R, R),
        key_gain.reshape(1, HD), queries,
        cache_keys.reshape(16 * ROWS, KVH * HD), cache_values.reshape(16 * ROWS, KVH * HD),
        cache_lengths, positions,
    ))
    return (attended, na.reshape(2, R, DS), nb.reshape(2, R, R))


def solution(mesh):
    return jax.shard_map(
        per_device,
        mesh=mesh,
        in_specs=(
            P("dp", None, "tensor"),
            P(None, "tensor", None),
            P(None, None, "tensor"),
            P(None, None, "tensor"),
            P("dp", None, None, "tensor"),
            P("dp", None, None, "tensor"),
            P(),
            P(("dp", "tensor"), None, None),
            P(("dp", "tensor"), None, None),
            P(("dp", "tensor"), None, None),
            P(("dp", "tensor")),
            P(("dp", "tensor")),
        ),
        out_specs=(
            P(("dp", "tensor"), None, None),
            P(None, None, "tensor"),
            P(None, None, "tensor"),
        ),
        check_vma=False,
    )
```

time: 63.5 us -> 58.5 us (0.921)
  local copies, waits for them, and re-layouts: 4.29 us -> 0 us
  Pallas kernels: 58.4 us -> 57.7 us
    unnamed x5 -> x0, local copies, waits for them, and re-layouts: 4.29 us -> none
    pallas_call x1, Pallas kernels: 58.4 us -> 55.7 us  [transfers(): pl.pallas_call(body, out_shape=(jax.ShapeDtypeStruct((ROWS, STEPS, QH * H...]
    pallas_call x0 -> x1, Pallas kernels: none -> 1.98 us  [results(): pl.pallas_call(results_kernel, out_shape=tuple((jax.ShapeDtypeStruct(x.sh...]
where the time goes in v3:
time: 58.5 us; the launch traced here: 58.3 us
  Pallas kernels  57.7 us (99%)
  between operations  0.64 us (1%)
    pallas_call x1, Pallas kernels, transfers(): pl.pallas_call(body, out_shape=(jax.ShapeDtypeStruct((ROWS, STEPS, QH * H...  55.7 us
    pallas_call x1, Pallas kernels, results(): pl.pallas_call(results_kernel, out_shape=tuple((jax.ShapeDtypeStruct(x.sh...  1.98 us

profile of v3, /device:TPU:1, one launch (start us, length us, event | category | flops | bytes accessed | tf_op | source)
XLA Modules:
  0.0 58.3 jit_solution(2966590333070248861)
XLA Ops:
  0.6 55.7 %shard_map.139 = (bf16[15,4,4096]{2,1,0:T(4,128)(2,1)}, f32[128,320]{1,0:T(8,128)}, f32[128,64]{1,0:T(8,128)}) custom-call(bf16[4,320,240]{2,1,0:T(8,128)(2,1)} %bitcast.10, bf16[2,320,1024]{2,1,0:T(8,128)(2,1)} %refs_1_.1, f32[128,320]{1,0:T(8,128)} %bitcast.13, f32[128,64]{1,0:T(8,128)} %bitcast.15, f32[128,320]{1,0:T(8,128)} %bitcast.14, ...), custom_call_target="tpu_custom_call" | custom-call | tf_op jit(solution)/shard_map/pallas_call | solution.py:504
  56.3 2.0 %shard_map.140 = (bf16[15,4,4096]{2,1,0:T(4,128)(2,1)}, f32[128,320]{1,0:T(8,128)}, f32[128,64]{1,0:T(8,128)}) custom-call(bf16[15,4,4096]{2,1,0:T(4,128)(2,1)} %get-tuple-element.9.att, f32[128,320]{1,0:T(8,128)} %get-tuple-element.10.na, f32[128,64]{1,0:T(8,128)} %get-tuple-element.11.nb), custom_call_target="tpu_custom_call" | custom-call | tf_op jit(solution)/shard_map/pallas_call | solution.py:602

commit v4 on v3

--- a/solution.py
+++ b/solution.py
@@ -191,6 +191,21 @@
             (((1,), (1,)), ((), ())), preferred_element_type=F32,
         )
 
+    usent = {}
+
+    def ustage(s):
+        if s == 0:
+            sbu[0, 0] = pu[0:TOK, :].astype(BF)
+            usent[0, 0] = remote(sbu.at[0, 0], rbu.at[0, 0], ring[0])
+            return
+        for way in range(2):
+            total = pu[(2 * s - 1 + way) * TOK:(2 * s + way) * TOK, :]
+            if s > 1 or way == 0:
+                usent[s - 1, way].wait_recv()
+                total = total + rbu[s - 1, way].astype(F32)
+            sbu[s, way] = total.astype(BF)
+            usent[s, way] = remote(sbu.at[s, way], rbu.at[s, way], ring[way])
+
     def prepare_masks():
         j = lax.broadcasted_iota(jnp.int32, (256, 256), 0)
         i = lax.broadcasted_iota(jnp.int32, (256, 256), 1)
@@ -293,22 +308,21 @@
     bmine = pl.ds(pl.multiple_of(DS + c * 32, 32), 32)
     btheirs = pl.ds(pl.multiple_of(DS + (1 - c) * 32, 32), 32)
     g1s[GH:, :] = gT[btheirs, :].astype(BF)
+    lw[1].wait()
+    lw[2].wait()
+    pl.semaphore_wait(barrier, len(peers))
+
+    g1 = remote(g1s, g1r, sib)
+    w1 = [weight(1, 0, 80, part), weight(1, 80, 80, other)]
+    w2 = weight(2, 0, 160, other)
     for cp in lh:
         cp.wait()
+    pick(1 - a, hsend)
+    hr = [hidden(i) for i in range(5)]
     pick(a, hown)
-    pick(1 - a, hsend)
     lw[0].wait()
     product(0, 0, TOK)
-    pl.semaphore_wait(barrier, len(peers))
-
-    g1 = remote(g1s, g1r, sib)
     stage(0, 0)
-    lw[1].wait()
-    w1 = [weight(1, 0, 80, part), weight(1, 80, 80, other)]
-    hr = [hidden(0)]
-    lw[2].wait()
-    w2 = weight(2, 0, 160, other)
-    hr += [hidden(i) for i in range(1, 5)]
 
     g1.wait_recv()
     h2[...] = (gT[pl.ds(mine, GH), :] + g1r[0:GH, :].astype(F32)).astype(BF)
@@ -422,10 +436,7 @@
     pu[...] = jnp.dot(hown[...], new_a(a), preferred_element_type=F32) + jnp.dot(
         hrem[...], new_a(1 - a), preferred_element_type=F32
     )
-    u1 = []
-    for i in range(7):
-        sbu[i] = pu[i * TOK:(i + 1) * TOK, :].astype(BF)
-        u1.append(remote(sbu.at[i], rbu.at[i], ypeer[ORDER[i]]))
+    ustage(0)
     for cp in b2:
         cp.wait_recv()
     nball[c, z, a] = (b2s[...] + b2r[0]).astype(BF)
@@ -435,13 +446,16 @@
     stage(1, 3)
     product(4, TOK, 7 * TOK)
     stage(4, 1)
+    ustage(1)
     product(3, 5 * TOK, 3 * TOK)
     stage(3, 2)
     cached(0)
     stage(2, 3)
     cached(1)
 
+    ustage(2)
     stage(4, 2)
+    ustage(3)
     stage(3, 3)
     for cp in b4:
         cp.wait_recv()
@@ -457,9 +471,9 @@
     lo_ += [local(nav, na)]
 
     u = pu[7 * TOK:, :]
-    for i in range(7):
-        u1[i].wait_recv()
-        u = u + rbu[i].astype(F32)
+    for way in range(2):
+        usent[3, way].wait_recv()
+        u = u + rbu[3, way].astype(F32)
     u = u * 0.25
     lane = lax.broadcasted_iota(jnp.int32, u.shape, 1)
     us = [jnp.where(lane >> 6 == p, u, 0.0).astype(BF) for p in range(2)]
@@ -534,8 +548,8 @@
             pltpu.VMEM((TOK, 256), BF),
             pltpu.VMEM((TOK, 256), BF),
             pltpu.VMEM((8 * TOK, 128), F32),
-            pltpu.VMEM((7, TOK, 128), BF),
-            pltpu.VMEM((7, TOK, 128), BF),
+            pltpu.VMEM((4, 2, TOK, 128), BF),
+            pltpu.VMEM((4, 2, TOK, 128), BF),
             pltpu.VMEM((2 * R, DS), F32),
             pltpu.VMEM((2 * R, R), F32),
             pltpu.VMEM((2 * R, DS), F32),

time: 58.5 us -> 57.2 us (0.978)
  Pallas kernels: 57.7 us -> 56.4 us
    pallas_call x1, Pallas kernels: 55.7 us -> 54.4 us  [transfers(): pl.pallas_call(body, out_shape=(jax.ShapeDtypeStruct((ROWS, STEPS, QH * H...]
where the time goes in v4:
time: 57.2 us; the launch traced here: 57.1 us
  Pallas kernels  56.4 us (99%)
  between operations  0.64 us (1%)
    pallas_call x1, Pallas kernels, transfers(): pl.pallas_call(body, out_shape=(jax.ShapeDtypeStruct((ROWS, STEPS, QH * H...  54.4 us
    pallas_call x1, Pallas kernels, results(): pl.pallas_call(results_kernel, out_shape=tuple((jax.ShapeDtypeStruct(x.sh...  1.98 us

profile of v4, /device:TPU:1, one launch (start us, length us, event | category | flops | bytes accessed | tf_op | source)
XLA Modules:
  0.0 57.1 jit_solution(14757631612475027678)
XLA Ops:
  0.6 54.4 %shard_map.139 = (bf16[15,4,4096]{2,1,0:T(4,128)(2,1)}, f32[128,320]{1,0:T(8,128)}, f32[128,64]{1,0:T(8,128)}) custom-call(bf16[4,320,240]{2,1,0:T(8,128)(2,1)} %bitcast.10, bf16[2,320,1024]{2,1,0:T(8,128)(2,1)} %refs_1_.1, f32[128,320]{1,0:T(8,128)} %bitcast.13, f32[128,64]{1,0:T(8,128)} %bitcast.15, f32[128,320]{1,0:T(8,128)} %bitcast.14, ...), custom_call_target="tpu_custom_call" | custom-call | tf_op jit(solution)/shard_map/pallas_call | solution.py:518
  55.1 2.0 %shard_map.140 = (bf16[15,4,4096]{2,1,0:T(4,128)(2,1)}, f32[128,320]{1,0:T(8,128)}, f32[128,64]{1,0:T(8,128)}) custom-call(bf16[15,4,4096]{2,1,0:T(4,128)(2,1)} %get-tuple-element.9.att, f32[128,320]{1,0:T(8,128)} %get-tuple-element.10.na, f32[128,64]{1,0:T(8,128)} %get-tuple-element.11.nb), custom_call_target="tpu_custom_call" | custom-call | tf_op jit(solution)/shard_map/pallas_call | solution.py:616

commit v5 on v4

--- a/solution.py
+++ b/solution.py
@@ -479,17 +479,18 @@
     us = [jnp.where(lane >> 6 == p, u, 0.0).astype(BF) for p in range(2)]
     x0.wait_recv()
     b5.wait_recv()
-    back = jnp.concatenate(
-        [nball[0, y, a].astype(F32), nball[1, y, a].astype(F32), jnp.zeros((64, 128), F32)], axis=0
-    ).T
-    nbv[...] = back[:, 0:R]
-    lo_ += [local(nbv, nb)]
     allb = [
         jnp.concatenate([nball[core, i, side] for i in range(NY) for core in range(2)], axis=0)
         for side in range(2)
     ]
     new_keys(0, first[...] + xr[...].astype(F32) + adapter(0))
     for k in range(1, NC):
+        if k == 3:
+            back = jnp.concatenate(
+                [nball[0, y, a].astype(F32), nball[1, y, a].astype(F32), jnp.zeros((64, 128), F32)], axis=0
+            ).T
+            nbv[...] = back[:, 0:R]
+            lo_ += [local(nbv, nb)]
         total = last(k)
         for n, j in enumerate(PIECES[k]):
             x = total[:, n * 256:n * 256 + 256] + adapter(j)

time: 57.2 us -> 57.2 us (level)
  no operation moved by 1% of the time
where the time goes in v5:
time: 57.2 us; the launch traced here: 57.1 us
  Pallas kernels  56.4 us (99%)
  between operations  0.64 us (1%)
    pallas_call x1, Pallas kernels, transfers(): pl.pallas_call(body, out_shape=(jax.ShapeDtypeStruct((ROWS, STEPS, QH * H...  54.4 us
    pallas_call x1, Pallas kernels, results(): pl.pallas_call(results_kernel, out_shape=tuple((jax.ShapeDtypeStruct(x.sh...  1.98 us

profile of v5, /device:TPU:1, one launch (start us, length us, event | category | flops | bytes accessed | tf_op | source)
XLA Modules:
  0.0 57.1 jit_solution(12566109153138279127)
XLA Ops:
  0.6 54.4 %shard_map.139 = (bf16[15,4,4096]{2,1,0:T(4,128)(2,1)}, f32[128,320]{1,0:T(8,128)}, f32[128,64]{1,0:T(8,128)}) custom-call(bf16[4,320,240]{2,1,0:T(8,128)(2,1)} %bitcast.10, bf16[2,320,1024]{2,1,0:T(8,128)(2,1)} %refs_1_.1, f32[128,320]{1,0:T(8,128)} %bitcast.13, f32[128,64]{1,0:T(8,128)} %bitcast.15, f32[128,320]{1,0:T(8,128)} %bitcast.14, ...), custom_call_target="tpu_custom_call" | custom-call | tf_op jit(solution)/shard_map/pallas_call | solution.py:519
  55.1 2.0 %shard_map.140 = (bf16[15,4,4096]{2,1,0:T(4,128)(2,1)}, f32[128,320]{1,0:T(8,128)}, f32[128,64]{1,0:T(8,128)}) custom-call(bf16[15,4,4096]{2,1,0:T(4,128)(2,1)} %get-tuple-element.9.att, f32[128,320]{1,0:T(8,128)} %get-tuple-element.10.na, f32[128,64]{1,0:T(8,128)} %get-tuple-element.11.nb), custom_call_target="tpu_custom_call" | custom-call | tf_op jit(solution)/shard_map/pallas_call | solution.py:617
